TPU v7x, 128 devices: a whole 4x4x4 slice. The times are simulated.
128 devices in a mesh: wide: 16 (over x, y_hi, core), narrow: 8 (over y_lo, z).
Axes of the slice: x: 4, y: 4 (y_hi: 2, y_lo: 2; y = y_hi * 2 + y_lo), z: 4, core: 2. Of those that a mesh axis runs over, the one named last changes fastest.
Arguments:
- field: float32 [20, 256, 256, 256], P(None, 'wide', 'narrow'), may hold values from -6 to 6
- spec_weight: float32 [1, 2, 20, 20, 48, 1152], P(None, None, None, None, 'wide', 'narrow'), may hold values from -8 to 8
- lin_weight: float32 [1, 20, 20], replicated, may hold values from -1.25 to 1.25
- bias: float32 [1, 20], replicated, may hold values from -3 to 3
Outputs:
- result: float32 [20, 256, 256, 256], P(None, 'wide', 'narrow')
All inputs are finite; a program needn't handle non-finite values.
Results may differ from a plain program's by a relative error of at most 0.0001.
Values sent between devices are 32-bit elements; how exact they have to be, the bound alone decides.
No kernel may reach another device: no remote copies, remote signals or barrier semaphores. Data moves between devices by JAX's collectives and lax.ppermute only.
A program may use at most 128 MiB of HBM per device.

v0:
```python
import math

import jax
import jax.numpy as jnp
from jax import lax
from jax.sharding import PartitionSpec as P

N = 256
MX = 48
MY = 48
MZ = 24


highest = lax.Precision.HIGHEST


def contract(form, left, right):
    return jnp.einsum(form, left, right, precision=highest)


def tables(length, freqs):
    places = jnp.arange(length, dtype=jnp.int32)
    phase = jnp.mod(freqs[:, None] * places[None, :], length)
    angle = phase.astype(jnp.float32) * (2.0 * math.pi / length)
    return (jnp.cos(angle), jnp.sin(angle))


def signed_freqs(count):
    half = count // 2
    upward = jnp.arange(half, dtype=jnp.int32)
    return jnp.concatenate([upward, upward - half])


def forward_rows(spec, cosine, sine):
    real_part, imag_part = (spec[0], spec[1])
    out_real = contract("ky,ayq->akq", cosine, real_part) + contract("ky,ayq->akq", sine, imag_part)
    out_imag = contract("ky,ayq->akq", cosine, imag_part) - contract("ky,ayq->akq", sine, real_part)
    return jnp.stack([out_real, out_imag])


def inverse_rows(spec, cosine, sine):
    real_part, imag_part = (spec[0], spec[1])
    out_real = contract("ky,akq->ayq", cosine, real_part) - contract("ky,akq->ayq", sine, imag_part)
    out_imag = contract("ky,akq->ayq", sine, real_part) + contract("ky,akq->ayq", cosine, imag_part)
    return jnp.stack([out_real, out_imag]) / N


def body(field, spec_weight, lin_weight, bias):
    wide_count = lax.axis_size("wide")
    narrow_count = lax.axis_size("narrow")
    channels, y_local, z_local, _ = field.shape
    mx_local = MX // wide_count
    my_local = MY // narrow_count
    cos_x, sin_x = tables(N, signed_freqs(MX))
    cos_y, sin_y = tables(N, signed_freqs(MY))
    cos_z, sin_z = tables(N, jnp.arange(MZ, dtype=jnp.int32))
    z_scale = jnp.where(jnp.arange(MZ) == 0, 1.0, 2.0).astype(jnp.float32)[:, None] / N
    back_cos_z = cos_z * z_scale
    back_sin_z = sin_z * z_scale
    hidden = field
    x_real = contract("cyzx,kx->kycz", hidden, cos_x)
    x_imag = -contract("cyzx,kx->kycz", hidden, sin_x)
    flat = jnp.stack([x_real, x_imag]).reshape(2, MX, y_local, channels * z_local)
    moved = lax.all_to_all(flat, "wide", split_axis=1, concat_axis=2, tiled=True)
    rows = forward_rows(moved, cos_y, sin_y)
    moved = lax.all_to_all(rows, "narrow", split_axis=2, concat_axis=3, tiled=True)
    moved = moved.reshape(2, mx_local, my_local, narrow_count, channels, z_local)
    cos_block = cos_z.reshape(MZ, narrow_count, z_local)
    sin_block = sin_z.reshape(MZ, narrow_count, z_local)
    mode_real = contract("abncz,knz->cabk", moved[0], cos_block) + contract(
        "abncz,knz->cabk", moved[1], sin_block
    )
    mode_imag = contract("abncz,knz->cabk", moved[1], cos_block) - contract(
        "abncz,knz->cabk", moved[0], sin_block
    )
    mode_real = mode_real.reshape(channels, mx_local, my_local * MZ)
    mode_imag = mode_imag.reshape(channels, mx_local, my_local * MZ)
    weights = spec_weight[0]
    mixed_real = contract("iam,ioam->oam", mode_real, weights[0]) - contract(
        "iam,ioam->oam", mode_imag, weights[1]
    )
    mixed_imag = contract("iam,ioam->oam", mode_real, weights[1]) + contract(
        "iam,ioam->oam", mode_imag, weights[0]
    )
    mixed_real = mixed_real.reshape(channels, mx_local, my_local, MZ)
    mixed_imag = mixed_imag.reshape(channels, mx_local, my_local, MZ)
    cos_block = back_cos_z.reshape(MZ, narrow_count, z_local)
    sin_block = back_sin_z.reshape(MZ, narrow_count, z_local)
    cells_real = contract("cabk,knz->abncz", mixed_real, cos_block) - contract(
        "cabk,knz->abncz", mixed_imag, sin_block
    )
    cells_imag = contract("cabk,knz->abncz", mixed_real, sin_block) + contract(
        "cabk,knz->abncz", mixed_imag, cos_block
    )
    flat = jnp.stack([cells_real, cells_imag]).reshape(
        2, mx_local, my_local, narrow_count * channels * z_local
    )
    moved = lax.all_to_all(flat, "narrow", split_axis=3, concat_axis=2, tiled=True)
    rows = inverse_rows(moved, cos_y, sin_y)
    moved = lax.all_to_all(rows, "wide", split_axis=2, concat_axis=1, tiled=True)
    planes = moved.reshape(2, MX, y_local, channels, z_local)
    spatial = (
        contract("kycz,kx->cyzx", planes[0], cos_x) - contract("kycz,kx->cyzx", planes[1], sin_x)
    ) / N
    linear = contract("io,iyzx->oyzx", lin_weight[0], hidden) + bias[0][:, None, None, None]
    hidden = jax.nn.gelu(spatial + linear, approximate=False)
    return hidden


def solution(mesh):
    placed = (
        P(None, "wide", "narrow", None),
        P(None, None, None, None, "wide", "narrow"),
        P(),
        P(),
    )
    return jax.shard_map(
        body, mesh=mesh, in_specs=placed, out_specs=P(None, "wide", "narrow", None), check_vma=False
    )
```

profile of v0, /device:TPU:17, one launch (start us, length us, event | category | flops | bytes accessed | tf_op | source)
XLA Modules:
  0.0 438.3 jit_solution(9743054782272103)
XLA Ops:
  0.1 14.0 %negate_bitcast_fusion = f32[48,16,20,32]{0,3,1,2:T(8,128)S(1)} fusion(f32[20,16,32,256]{3,2,1,0:T(8,128)} %param.4, s32[48]{0:T(128)S(1)} %pad_add_fusion), kind=kOutput, calls=%fused_computation.23 | convolution fusion | flops 1510612992 | bytes 12452032 | tf_op jit(solution)/shard_map/cyzx,kx->kycz/dot_general | solution.py:18
  14.1 9.7 %convolution_bitcast_fusion = f32[48,16,20,32]{0,3,1,2:T(8,128)S(1)} fusion(f32[20,16,32,256]{3,2,1,0:T(8,128)S(1)} %copy-done, s32[48]{0:T(128)S(1)} %pad_add_fusion), kind=kOutput, calls=%fused_computation.25 | convolution fusion | flops 1510121472 | bytes 12452032 | tf_op jit(solution)/shard_map/cyzx,kx->kycz/dot_general | solution.py:18
  25.3 4.8 %pad_maximum_fusion = f32[2,48,16,640]{1,3,2,0:T(8,128)} fusion(f32[1,48,16,640]{1,3,2,0:T(8,128)S(1)} %bitcast.227, f32[1,48,16,640]{1,3,2,0:T(8,128)S(1)} %bitcast.228), kind=kLoop, calls=%fused_computation.5 | loop fusion | flops 983040 | bytes 7864320 | tf_op jit(solution)/shard_map/stack | solution.py:63
  30.2 9.1 %copy.137 = f32[2,48,16,640]{3,2,0,1:T(8,128)} copy(f32[2,48,16,640]{1,3,2,0:T(8,128)} %pad_maximum_fusion) | data formatting | bytes 7864320 | tf_op jit(solution)/shard_map/stack | solution.py:63
  39.3 54.1 %all_to_all.60 = f32[2,48,16,640]{3,2,0,1:T(8,128)S(1)} all-to-all(f32[2,48,16,640]{3,2,0,1:T(8,128)} %copy.137), channel_id=1, replica_groups=mesh['wide'=16,'narrow'=8] {'wide'}, dimensions={1} | all-to-all | bytes 7864320 | tf_op jit(solution)/shard_map/all_to_all | solution.py:64
  101.7 5.9 %all-to-all-start.1 = ((f32[2,3,48,640]{3,0,1,2:T(2,128)}), f32[2,3,48,640]{3,0,1,2:T(2,128)S(1)}, u32[]{:S(2)}, u32[]{:S(2)}) async-start(f32[2,3,48,640]{3,0,1,2:T(2,128)} %copy.141), calls=%async_computation.1 | async-start | bytes 1474560 | tf_op jit(solution)/shard_map/all_to_all | solution.py:66
  107.6 3.3 fusion.185
  110.9 7.8 %all-to-all-done.1 = f32[2,3,48,640]{3,0,1,2:T(2,128)S(1)} async-done(((f32[2,3,48,640]{3,0,1,2:T(2,128)}), f32[2,3,48,640]{3,0,1,2:T(2,128)S(1)}, u32[]{:S(2)}, u32[]{:S(2)}) %all-to-all-start.1) | async-done | bytes 737312 | tf_op jit(solution)/shard_map/all_to_all | solution.py:66
  122.6 4.7 %convolution_bitcast_fusion.3 = f32[24,3,6,20]{3,0,2,1:T(8,128)S(1)} fusion(f32[3,6,8,20,32]{4,3,2,1,0:T(8,128)S(1)} %squeeze.41, s32[8,32]{1,0:T(8,128)S(1)} %multiply_add_fusion), kind=kOutput, calls=%fused_computation.46 | convolution fusion | flops 26628096 | bytes 404224 | tf_op jit(solution)/shard_map/abncz,knz->cabk/dot_general | solution.py:18
  127.3 4.7 %convolution_bitcast_fusion.1 = f32[24,3,6,20]{3,0,2,1:T(8,128)S(1)} fusion(f32[3,6,8,20,32]{4,3,2,1,0:T(8,128)S(1)} %squeeze.40, s32[8,32]{1,0:T(8,128)S(1)} %multiply_add_fusion), kind=kOutput, calls=%fused_computation.44 | convolution fusion | flops 26628096 | bytes 404224 | tf_op jit(solution)/shard_map/abncz,knz->cabk/dot_general | solution.py:18
  132.0 5.5 %fusion.21 = f32[24,3,6,20]{3,0,2,1:T(8,128)} fusion(f32[24,3,6,20]{3,0,2,1:T(8,128)S(1)} %convolution_bitcast_fusion.3, f32[3,6,8,20,32]{4,3,2,1,0:T(8,128)S(1)} %squeeze.40, s32[8,32]{1,0:T(8,128)S(1)} %multiply_add_fusion), kind=kOutput, calls=%fused_computation.48 | convolution fusion | flops 26636736 | bytes 438784 | tf_op jit(solution)/shard_map/abncz,knz->cabk/dot_general | solution.py:18
  137.8 4.7 %fusion.22 = f32[24,3,6,20]{3,0,2,1:T(8,128)S(1)} fusion(f32[24,3,6,20]{3,0,2,1:T(8,128)S(1)} %convolution_bitcast_fusion.1, f32[3,6,8,20,32]{4,3,2,1,0:T(8,128)S(1)} %squeeze.41, s32[8,32]{1,0:T(8,128)S(1)} %multiply_add_fusion), kind=kOutput, calls=%fused_computation.49 | convolution fusion | flops 26636736 | bytes 438784 | tf_op jit(solution)/shard_map/abncz,knz->cabk/dot_general | solution.py:18
  158.6 2.9 subtract_bitcast_fusion.1
  163.4 14.3 %copy.153 = f32[2,3,6,5120]{2,0,1,3:T(2,128)} copy(f32[2,3,6,5120]{3,2,1,0:T(8,128)S(1)} %pad_maximum_fusion.1) | data formatting | bytes 1474560 | tf_op jit(solution)/shard_map/stack | solution.py:95
  177.7 25.6 %reshape.237 = f32[8,1,23040]{2,1,0:T(1,128)S(1)} reshape(f32[5120,3,2,6]{3,2,1,0:T(2,128)} %bitcast.224) | data formatting | bytes 1474560
  203.3 15.0 %all_to_all.61 = f32[8,1,23040]{2,1,0:T(1,128)S(1)} all-to-all(f32[8,1,23040]{2,1,0:T(1,128)S(1)} %reshape.237), channel_id=1, replica_groups=mesh['wide'=16,'narrow'=8] {'narrow'}, dimensions={0} | all-to-all | bytes 1474560 | tf_op jit(solution)/shard_map/all_to_all | solution.py:98
  221.2 29.8 %reshape.238 = f32[5120,3,2,6]{3,2,1,0:T(2,128)} reshape(f32[8,23040]{1,0:T(8,128)S(1)} %reduce.8) | data formatting | bytes 1474560
  251.1 12.8 %copy.206 = f32[2,3,6,8,640]{4,3,0,2,1:T(8,128)S(1)} copy(f32[2,3,6,8,640]{2,0,1,4,3:T(2,128)} %bitcast.223) | data formatting | bytes 1474560 | tf_op jit(solution)/shard_map/all_to_all | solution.py:98
  264.1 3.2 fusion.56
  269.4 3.5 add_bitcast_fusion
  277.2 7.8 %copy.157 = f32[2,3,256,640]{3,0,1,2:T(2,128)} copy(f32[2,3,256,640]{2,3,1,0:T(8,128)} %maximum_multiply_fusion) | data formatting | bytes 7864320 | tf_op jit(solution)/shard_map/div | solution.py:45
  285.0 8.1 %all-to-all-start.3 = ((f32[2,3,256,640]{3,0,1,2:T(2,128)}), f32[2,3,256,640]{3,0,1,2:T(2,128)}, u32[]{:S(2)}, u32[]{:S(2)}) async-start(f32[2,3,256,640]{3,0,1,2:T(2,128)} %copy.157), calls=%async_computation.3 | async-start | bytes 7864320 | tf_op jit(solution)/shard_map/all_to_all | solution.py:100
  293.2 22.8 %fusion = f32[20,16,32,256]{3,0,2,1:T(8,128)} fusion(f32[20,16,32,256]{3,2,1,0:T(8,128)} %param.4, f32[1,20,20]{1,2,0:T(8,128)S(1)} %copy.207), kind=kOutput, calls=%fused_computation.1 | convolution fusion | flops 629145600 | bytes 20973120 | tf_op jit(solution)/shard_map/io,iyzx->oyzx/dot_general | solution.py:18
  316.0 31.1 %all-to-all-done.3 = f32[2,3,256,640]{3,0,1,2:T(2,128)} async-done(((f32[2,3,256,640]{3,0,1,2:T(2,128)}), f32[2,3,256,640]{3,0,1,2:T(2,128)}, u32[]{:S(2)}, u32[]{:S(2)}) %all-to-all-start.3) | async-done | bytes 3932192 | tf_op jit(solution)/shard_map/all_to_all | solution.py:100
  351.5 6.7 %squeeze.46 = f32[48,16,20,32]{3,2,1,0:T(8,128)} reshape(f32[1,16,3,16,640]{4,3,2,1,0:T(8,128)} %copy.159) | data formatting | bytes 3932160 | tf_op jit(solution)/shard_map/squeeze | solution.py:103
  358.2 9.3 %copy.160 = f32[48,16,20,32]{0,3,2,1:T(8,128)} copy(f32[48,16,20,32]{3,2,1,0:T(8,128)} %squeeze.46) | data formatting | bytes 3932160 | tf_op jit(solution)/shard_map/squeeze | solution.py:103
  367.5 13.3 %fusion.90 = f32[256,10240]{0,1} fusion(f32[48,10240]{0,1:T(8,128)} %bitcast.230, s32[48]{0:T(128)S(1)} %pad_add_fusion), kind=kOutput, calls=%fused_computation.116 | convolution fusion | flops 1510121472 | bytes 12452032
  380.8 5.2 %squeeze.47 = f32[48,16,20,32]{3,2,1,0:T(8,128)} reshape(f32[1,16,3,16,640]{4,3,2,1,0:T(8,128)S(1)} %copy.161) | data formatting | bytes 3932160 | tf_op jit(solution)/shard_map/squeeze | solution.py:103
  386.0 9.3 %copy.162 = f32[48,16,20,32]{0,3,2,1:T(8,128)} copy(f32[48,16,20,32]{3,2,1,0:T(8,128)} %squeeze.47) | data formatting | bytes 3932160 | tf_op jit(solution)/shard_map/squeeze | solution.py:103
  395.3 10.9 %fusion.97 = f32[256,10240]{0,1:S(1)} fusion(f32[48,10240]{0,1:T(8,128)} %bitcast.229, s32[48]{0:T(128)S(1)} %pad_add_fusion), kind=kOutput, calls=%fused_computation.117 | convolution fusion | flops 1510121472 | bytes 12452032
  406.2 26.6 %fusion.3 = f32[20,16,32,256]{3,2,0,1:T(8,128)S(1)} fusion(f32[20,16,32,256]{3,0,2,1:T(8,128)} %fusion, f32[256,16,20,32]{0,3,2,1:T(8,128)S(1)} %bitcast.225, f32[256,16,20,32]{0,3,2,1:T(8,128)S(1)} %bitcast.226, f32[20]{0:T(128)S(1)} %bitcast.241), kind=kLoop, calls=%fused_computation.4 | loop fusion | flops 178257920 | bytes 41943120 | tf_op jit(solution)/shard_map/mul | solution.py:106
  432.9 5.2 %copy.166 = f32[20,16,32,256]{3,2,1,0:T(8,128)} copy(f32[20,16,32,256]{3,2,0,1:T(8,128)S(1)} %fusion.3) | data formatting | bytes 20971520 | tf_op jit(solution)/shard_map/mul | solution.py:106
  (64 shorter events, 45.4 us)
Async XLA Ops:
  0.0 14.1 %copy-start = (f32[20,16,32,256]{3,2,1,0:T(8,128)S(1)}, f32[20,16,32,256]{3,2,1,0:T(8,128)}, u32[]{:S(2)}) copy-start(f32[20,16,32,256]{3,2,1,0:T(8,128)} %param.4) | copy-start | bytes 31457284
  93.9 13.7 %copy-start.2 = (f32[1,2,20,20,3,144]{5,1,4,3,2,0:T(2,128)S(1)}, f32[1,2,20,20,3,144]{5,1,4,3,2,0:T(2,128)}, u32[]{:S(2)}) copy-start(f32[1,2,20,20,3,144]{5,1,4,3,2,0:T(2,128)} %param.5) | copy-start | bytes 4147204
  101.7 17.1 %all-to-all-start.1 = ((f32[2,3,48,640]{3,0,1,2:T(2,128)}), f32[2,3,48,640]{3,0,1,2:T(2,128)S(1)}, u32[]{:S(2)}, u32[]{:S(2)}) async-start(f32[2,3,48,640]{3,0,1,2:T(2,128)} %copy.141), calls=%async_computation.1 | async-start | bytes 1474560 | tf_op jit(solution)/shard_map/all_to_all | solution.py:66
  147.0 0.7 copy-start.3
  275.0 18.1 %copy-start.4 = (f32[1,20,20]{2,0,1:T(1,128)S(1)}, f32[1,20,20]{2,0,1:T(1,128)}, u32[]{:S(2)}) copy-start(f32[1,20,20]{2,0,1:T(1,128)} %param.6) | copy-start | bytes 4804
  285.0 62.1 %all-to-all-start.3 = ((f32[2,3,256,640]{3,0,1,2:T(2,128)}), f32[2,3,256,640]{3,0,1,2:T(2,128)}, u32[]{:S(2)}, u32[]{:S(2)}) async-start(f32[2,3,256,640]{3,0,1,2:T(2,128)} %copy.157), calls=%async_computation.3 | async-start | bytes 7864320 | tf_op jit(solution)/shard_map/all_to_all | solution.py:100
  395.3 10.9 %copy-start.1 = (f32[256,10240]{0,1:S(1)}, f32[256,10240]{0,1}, u32[]{:S(2)}) copy-start(f32[256,10240]{0,1} %fusion.90) | copy-start | bytes 31457284
  395.3 10.9 %copy-start.5 = (f32[1,20]{1,0:T(1,128)S(1)}, f32[1,20]{1,0:T(1,128)}, u32[]{:S(2)}) copy-start(f32[1,20]{1,0:T(1,128)} %param.7) | copy-start | bytes 244
where the time goes:
time: 444 us; the launch traced here: 438 us
  local copies, waits for them, and re-layouts  158 us (36%)
  matrix products  117 us (26%)
  blocking collectives  69.1 us (16%)
  other arithmetic  40.4 us (9%)
  waiting for transfers between devices  38.9 us (9%)
  starting transfers between devices  14 us (3%)
    dot_general x19, matrix products, contract(): return jnp.einsum(form, left, right, precision=highest)  93.2 us
    unnamed x16, local copies, waits for them, and re-layouts  57.5 us
    all_to_all x1, blocking collectives, body(): lax.all_to_all(flat, 'wide', split_axis=1, concat_axis=2, tiled=True)  54.1 us
    all_to_all x1, waiting for transfers between devices, body(): lax.all_to_all(rows, 'wide', split_axis=2, concat_axis=1, tiled=True)  31.1 us
    mul x1, other arithmetic, body(): hidden = jax.nn.gelu(spatial + linear, approximate=False)  26.6 us
    unnamed x2, matrix products  24.1 us
    another operation x3, local copies, waits for them, and re-layouts, body(): jnp.stack([cells_real, cells_imag])  16.4 us
    squeeze x2, local copies, waits for them, and re-layouts, body(): planes[0]  16 us
  transfers between devices with their start and end apart: 2, of which 2 were waited for; matrix products, arithmetic and copies ran while one was open for 6% of the time, Pallas kernels for 0%

commit v1 on v0

v1 whole, which is shorter than its diff:
```python
import functools

import jax
import jax.numpy as jnp
import ml_dtypes
import numpy as np
from jax import lax
from jax.experimental import pallas as pl
from jax.experimental.pallas import tpu as pltpu
from jax.sharding import PartitionSpec as P

N = 256
C = 20
MX = 48
MY = 48
MZ = 24
WIDE = 16
NARROW = 8
HALF = 24
SEQS = 49
GROUPS = 4
LANES = GROUPS * 128
ROWS = 40

f32 = jnp.float32
bf16 = jnp.bfloat16


def signed(count):
    half = count // 2
    return np.concatenate([np.arange(half), np.arange(half) - half])


def halves(table):
    high = table.astype(ml_dtypes.bfloat16)
    low = (table - high.astype(np.float64)).astype(ml_dtypes.bfloat16)
    return high, low


def x_table():
    angle = 2 * np.pi * (np.outer(np.arange(HALF + 1), np.arange(N)) % N) / N
    table = np.zeros((64, N))
    table[: HALF + 1] = np.cos(angle)
    table[HALF + 1 : SEQS] = np.sin(angle[1:])
    return table


def z_tables(scale):
    angle = 2 * np.pi * np.outer(np.arange(32), np.arange(MZ)) / N
    table = np.zeros((GROUPS, 256, 2, 128))
    for group in range(GROUPS):
        for channel in range(5):
            rows = slice(32 * group + 32 * channel, 32 * group + 32 * channel + 32)
            lanes = slice(MZ * channel, MZ * channel + MZ)
            table[group, rows, 0, lanes] = np.cos(angle) * scale
            table[group, rows, 1, lanes] = np.sin(angle) * scale
    return table


def phase_table():
    angle = 2 * np.pi * (np.outer(np.arange(NARROW), np.arange(MZ)) % 8) / 8
    table = np.zeros((NARROW, 2, 128), np.float32)
    for channel in range(5):
        table[:, 0, MZ * channel : MZ * channel + MZ] = np.cos(angle)
        table[:, 1, MZ * channel : MZ * channel + MZ] = np.sin(angle)
    return table


def y_tables():
    angle = 2 * np.pi * (np.outer(signed(MY), np.arange(N)) % N) / N
    cosine = np.cos(angle).reshape(NARROW, 6, WIDE, 2, 8)
    sine = np.sin(angle).reshape(NARROW, 6, WIDE, 2, 8)
    forward = np.zeros((NARROW, ROWS, WIDE, 2, 3, 2, 8))
    backward = np.zeros((WIDE, 2, 3, 2, 8, NARROW, ROWS))
    for ky in range(6):
        for kx in range(3):
            real, imag = 6 * ky + kx, 6 * ky + 3 + kx
            c, s = cosine[:, ky], sine[:, ky]
            forward[:, real, :, :, kx, 0] = c
            forward[:, real, :, :, kx, 1] = s
            forward[:, imag, :, :, kx, 0] = -s
            forward[:, imag, :, :, kx, 1] = c
            c, s = (np.moveaxis(t, 0, -1) / N for t in (c, s))
            backward[:, :, kx, 0, :, :, real] = c
            backward[:, :, kx, 0, :, :, imag] = -s
            backward[:, :, kx, 1, :, :, real] = s
            backward[:, :, kx, 1, :, :, imag] = c
    return (
        forward.reshape(NARROW * ROWS, WIDE * 96),
        backward.reshape(WIDE * 96, NARROW * ROWS),
    )


def split(value):
    high = value.astype(bf16)
    return high, (value - high.astype(f32)).astype(bf16)


def dot(left, right, contract=((1,), (0,))):
    return lax.dot_general(left, right, (contract, ((), ())), preferred_element_type=f32)


def dot3(left, right):
    return dot(left[0], right[0]) + dot(left[0], right[1]) + dot(left[1], right[0])


def forward_cells(x_ref, e_ref, zh_ref, zl_ref, phase_ref, out_ref, seq_ref):
    row = lax.rem(pl.program_id(0), 8)
    high, low = split(x_ref[...].reshape(C * 32, N))
    both = dot(e_ref[...], high, ((1,), (1,)))
    seqs = both[:56] + both[64:120] + dot(e_ref[:64], low, ((1,), (1,)))[:56]
    for tile in range(5):
        seq_ref[tile, pl.ds(row, 56, stride=8), :] = seqs[:, 128 * tile : 128 * tile + 128]

    @pl.when(row == 7)
    def _():
        turn = phase_ref[lax.axis_index("narrow")]
        turn_c, turn_s = turn[0:1], turn[1:2]
        for group in range(GROUPS):
            window = jnp.concatenate(
                [seq_ref[group, : SEQS * 8, :], seq_ref[group + 1, : SEQS * 8, :]], axis=1
            )
            modes = dot3(split(window), (zh_ref[group], zl_ref[group]))
            cosine, sine = modes[:, :128], modes[:, 128:]
            cosine, sine = turn_c * cosine - turn_s * sine, turn_s * cosine + turn_c * sine
            lanes = slice(128 * group, 128 * group + 128)
            for index in range(MX):
                freq = index if index < 24 else 48 - index
                at = slice(8 * freq, 8 * freq + 8)
                real, imag = cosine[at], -sine[at]
                if freq:
                    at = slice(8 * (24 + freq), 8 * (24 + freq) + 8)
                    if index < 24:
                        real, imag = real - sine[at], imag - cosine[at]
                    else:
                        real, imag = real + sine[at], imag + cosine[at]
                kx = 16 * (index % 3)
                out_ref[index // 3, kx : kx + 8, lanes] = real
                out_ref[index // 3, kx + 8 : kx + 16, lanes] = imag


def forward_rows(high_ref, low_ref, in_ref, out_ref):
    step = pl.program_id(0)
    part = dot3((high_ref[...], low_ref[...]), split(in_ref[...].reshape(-1, LANES)))
    part = part.reshape(NARROW, ROWS, LANES)

    @pl.when(step == 0)
    def _():
        out_ref[...] = part

    @pl.when(step > 0)
    def _():
        out_ref[...] += part


def mix(in_ref, w_ref, out_ref):
    total = jnp.sum(in_ref[...], axis=0)
    lane = lax.broadcasted_iota(jnp.int32, (8, 128), 1)
    rows = [total[6 * ky : 6 * ky + 8] for ky in range(5)]
    rows.append(jnp.concatenate([total[30:36], total[30:32]], axis=0))

    def roll(value, shift):
        shift = shift % 128
        return pltpu.roll(value, shift, 1) if shift else value

    spectra = []
    for channel in range(C):
        group, place = divmod(channel, 5)
        first = jnp.zeros((8, 128), f32)
        for ky in range(6):
            block = roll(rows[ky][:, 128 * group : 128 * group + 128], MZ * (ky - place))
            first = jnp.where(lane >= MZ * ky, block, first)
        spectra.append(jnp.concatenate([first, block], axis=1)[:, :144])
    mixed = []
    for start in range(0, C, 5):
        real = jnp.zeros((5, 3, 144), f32)
        imag = jnp.zeros((5, 3, 144), f32)
        for channel in range(C):
            a, b = spectra[channel][None, 0:3], spectra[channel][None, 3:6]
            u = w_ref[0, channel, start : start + 5]
            v = w_ref[1, channel, start : start + 5]
            real += a * u - b * v
            imag += a * v + b * u
        for place in range(5):
            mixed.append(jnp.concatenate([real[place], imag[place]], axis=0))
    lane = lane[:6]
    for group in range(GROUPS):
        for ky in range(6):
            tile = jnp.zeros((6, 128), f32)
            for place in range(5):
                value = mixed[5 * group + place]
                block = value[:, :128]
                if ky == 5:
                    rest = jnp.concatenate([value[:, 128:], jnp.zeros((6, 112), f32)], axis=1)
                    block = jnp.where(lane >= 120, block, rest)
                block = roll(block, MZ * (place - ky))
                inside = (lane >= MZ * place) & (lane < MZ * place + MZ)
                tile = jnp.where(inside, block, tile)
            for narrow in range(NARROW):
                out_ref[narrow, 6 * ky : 6 * ky + 6, 128 * group : 128 * group + 128] = tile
    for narrow in range(NARROW):
        out_ref[narrow, 36:40, :] = jnp.zeros((4, LANES), f32)


def backward_rows(high_ref, low_ref, in_ref, out_ref):
    part = dot3((high_ref[...], low_ref[...]), split(in_ref[...].reshape(-1, LANES)))
    out_ref[...] = part.reshape(out_ref.shape)


def gelu(value):
    return 0.5 * value * (1.0 + lax.erf(value * np.float32(np.sqrt(0.5))))


def backward_cells(
    x_ref, in_ref, eh_ref, el_ref, zh_ref, zl_ref, phase_ref, lin_ref, bias_ref, out_ref, cell_ref, lh_ref, ll_ref
):
    step = pl.program_id(0)
    row = lax.rem(step, 8)

    @pl.when(step == 0)
    def _():
        spread = lax.broadcasted_iota(jnp.int32, (160, C), 0) // 8
        spread = (spread == lax.broadcasted_iota(jnp.int32, (160, C), 1)).astype(bf16)
        rows = lax.broadcasted_iota(jnp.int32, (160, 160), 0)
        cols = lax.broadcasted_iota(jnp.int32, (160, 160), 1)
        same = (rows & 7) == (cols & 7)
        for part, ref in zip(split(lin_ref[...]), (lh_ref, ll_ref)):
            wide = dot(spread, part, ((1,), (1,))).astype(bf16)
            wide = dot(wide, spread, ((1,), (1,)))
            ref[...] = jnp.where(same, wide, 0.0).astype(bf16)

    @pl.when(row == 0)
    def _():
        base = 48 * (step // 8)
        turn = phase_ref[lax.axis_index("narrow")]
        turn_c, turn_s = turn[0:1], turn[1:2]
        carry = None
        for group in range(GROUPS):
            lanes = slice(128 * group, 128 * group + 128)

            def mode(index, part):
                at = base + 16 * (index % 3) + 8 * part
                return in_ref[index // 3, pl.ds(pl.multiple_of(at, 8), 8), lanes]

            first, second = [], []
            for freq in range(HALF + 1):
                if freq == 0:
                    u, v = mode(0, 0), mode(0, 1)
                elif freq == HALF:
                    u, v = mode(48 - freq, 0), mode(48 - freq, 1)
                else:
                    u = mode(freq, 0) + mode(48 - freq, 0)
                    v = mode(freq, 1) + mode(48 - freq, 1)
                first.append(u)
                second.append(v)
            for freq in range(1, HALF + 1):
                if freq == HALF:
                    u, v = mode(48 - freq, 1), -mode(48 - freq, 0)
                else:
                    u = mode(48 - freq, 1) - mode(freq, 1)
                    v = mode(freq, 0) - mode(48 - freq, 0)
                first.append(u)
                second.append(v)
            u, v = jnp.concatenate(first, axis=0), jnp.concatenate(second, axis=0)
            u, v = turn_c * u - turn_s * v, turn_s * u + turn_c * v
            cells = dot3(split(jnp.concatenate([u, v], axis=1)), (zh_ref[group], zl_ref[group]))
            left, right = cells[:, :128], cells[:, 128:]
            cell_ref[group, : SEQS * 8, :] = left if carry is None else left + carry
            carry = right
        cell_ref[GROUPS, : SEQS * 8, :] = carry
        for tile in range(5):
            cell_ref[tile, SEQS * 8 :, :] = jnp.zeros((512 - SEQS * 8, 128), f32)

    seqs = jnp.concatenate(
        [cell_ref[tile, pl.ds(row, 64, stride=8), :] for tile in range(5)], axis=1
    )
    seqs = jnp.transpose(seqs)
    high, low = split(seqs)
    spatial = dot(high, eh_ref[...]) + dot(high, el_ref[...]) + dot(low, eh_ref[...])
    spatial = spatial.reshape(C, 32, N)
    for block in range(4):
        at = slice(8 * block, 8 * block + 8)
        high, low = split(x_ref[:, 0, at, :].reshape(C * 8, N))
        linear = dot(lh_ref[...], high) + dot(ll_ref[...], high) + dot(lh_ref[...], low)
        linear = linear.reshape(C, 8, N) + spatial[:, at]
        for channel in range(C):
            out_ref[channel, 0, at, :] = gelu(linear[channel] + bias_ref[0, channel])


def whole(shape):
    return pl.BlockSpec(shape, lambda *_: (0,) * len(shape))


def params(mib):
    return pltpu.CompilerParams(
        dimension_semantics=("arbitrary",), vmem_limit_bytes=mib * 1024 * 1024
    )


def body(field, spec_weight, lin_weight, bias):
    eh, el = halves(x_table())
    zh, zl = (t.reshape(GROUPS, 256, 256) for t in halves(z_tables(1.0)))
    phase = phase_table()
    cells = pl.pallas_call(
        forward_cells,
        grid=(16,),
        in_specs=[
            pl.BlockSpec((C, 1, 32, N), lambda y: (0, y, 0, 0)),
            whole((128, N)),
            whole((GROUPS, 256, 256)),
            whole((GROUPS, 256, 256)),
            whole((NARROW, 2, 128)),
        ],
        out_specs=pl.BlockSpec((WIDE, 48, LANES), lambda y: (0, y // 8, 0)),
        out_shape=jax.ShapeDtypeStruct((WIDE, 96, LANES), f32),
        scratch_shapes=[pltpu.VMEM((5, 512, 128), f32)],
        compiler_params=params(48),
        name="forward_cells",
    )(field, np.concatenate([eh, el]), zh, zl, phase)
    moved = lax.all_to_all(cells, "wide", split_axis=0, concat_axis=0, tiled=True)

    forward, backward = y_tables()
    forward, backward = halves(forward), halves(backward)
    rows = pl.pallas_call(
        forward_rows,
        grid=(4,),
        in_specs=[
            pl.BlockSpec((NARROW * ROWS, 384), lambda s: (0, s)),
            pl.BlockSpec((NARROW * ROWS, 384), lambda s: (0, s)),
            pl.BlockSpec((4, 96, LANES), lambda s: (s, 0, 0)),
        ],
        out_specs=whole((NARROW, ROWS, LANES)),
        out_shape=jax.ShapeDtypeStruct((NARROW, ROWS, LANES), f32),
        compiler_params=params(32),
        name="forward_rows",
    )(*forward, moved)
    moved = lax.all_to_all(rows, "narrow", split_axis=0, concat_axis=0, tiled=True)

    modes = pl.pallas_call(
        mix,
        out_shape=jax.ShapeDtypeStruct((NARROW, ROWS, LANES), f32),
        compiler_params=pltpu.CompilerParams(vmem_limit_bytes=32 * 1024 * 1024),
        name="mix",
    )(moved, spec_weight.reshape(2, C, C, 3, 144))
    moved = lax.all_to_all(modes, "narrow", split_axis=0, concat_axis=0, tiled=True)

    rows = pl.pallas_call(
        backward_rows,
        grid=(4,),
        in_specs=[
            pl.BlockSpec((384, NARROW * ROWS), lambda s: (s, 0)),
            pl.BlockSpec((384, NARROW * ROWS), lambda s: (s, 0)),
            whole((NARROW, ROWS, LANES)),
        ],
        out_specs=pl.BlockSpec((4, 96, LANES), lambda s: (s, 0, 0)),
        out_shape=jax.ShapeDtypeStruct((WIDE, 96, LANES), f32),
        compiler_params=params(32),
        name="backward_rows",
    )(*backward, moved)
    moved = lax.all_to_all(rows, "wide", split_axis=0, concat_axis=0, tiled=True)

    eh, el = halves(x_table() / N)
    scale = np.where(np.arange(MZ) == 0, 1.0, 2.0) / N
    table = z_tables(scale)
    table[:, :, 1] *= -1
    zh, zl = halves(table.reshape(GROUPS, 256, 256).transpose(0, 2, 1))
    return pl.pallas_call(
        backward_cells,
        grid=(16,),
        in_specs=[
            pl.BlockSpec((C, 1, 32, N), lambda y: (0, y, 0, 0)),
            whole((WIDE, 96, LANES)),
            whole((64, N)),
            whole((64, N)),
            whole((GROUPS, 256, 256)),
            whole((GROUPS, 256, 256)),
            whole((NARROW, 2, 128)),
            whole((C, C)),
            pl.BlockSpec(memory_space=pltpu.SMEM),
        ],
        out_specs=pl.BlockSpec((C, 1, 32, N), lambda y: (0, y, 0, 0)),
        out_shape=jax.ShapeDtypeStruct(field.shape, f32),
        scratch_shapes=[
            pltpu.VMEM((5, 512, 128), f32),
            pltpu.VMEM((160, 160), bf16),
            pltpu.VMEM((160, 160), bf16),
        ],
        compiler_params=params(48),
        name="backward_cells",
    )(field, moved, eh, el, zh, zl, phase, lin_weight.reshape(C, C), bias)


def solution(mesh):
    placed = (
        P(None, "wide", "narrow", None),
        P(None, None, None, None, "wide", "narrow"),
        P(),
        P(),
    )
    return jax.shard_map(
        body, mesh=mesh, in_specs=placed, out_specs=P(None, "wide", "narrow", None), check_vma=False
    )
```

time: 444 us -> 179 us (0.40)
  local copies, waits for them, and re-layouts: 158 us -> 8.29 us
  matrix products: 117 us -> 0 us
  Pallas kernels: 0 us -> 45.5 us
  other arithmetic: 40.4 us -> 0 us
  waiting for transfers between devices: 38.9 us -> 50.8 us
  blocking collectives: 69.1 us -> 59.5 us
    dot_general x19 -> x0, matrix products: 93.2 us -> none  [contract(): return jnp.einsum(form, left, right, precision=highest)]
    unnamed x16 -> x32, local copies, waits for them, and re-layouts: 57.5 us -> 8.29 us
    pallas_call x0 -> x5, Pallas kernels: none -> 45.5 us  [the longest x1 20.5 us: body(): pl.pallas_call(backward_cells, grid=(16,), in_specs=[pl.BlockSpec((C, 1,...]
    squeeze x9 -> x0, local copies, waits for them, and re-layouts: 32.9 us -> none  [the longest x2 16 us: body(): planes[0]]
    another operation x5 -> x0, local copies, waits for them, and re-layouts: 26.8 us -> none  [the longest x3 16.4 us: body(): jnp.stack([cells_real, cells_imag])]
    mul x2 -> x0, other arithmetic: 26.7 us -> none  [the longest x1 26.6 us: body(): hidden = jax.nn.gelu(spatial + linear, approximate=False)]
    unnamed x2 -> x0, matrix products: 24.1 us -> none
    all_to_all x5 -> x0, local copies, waits for them, and re-layouts: 16.2 us -> none  [the longest x2 13.3 us: body(): lax.all_to_all(flat, 'narrow', split_axis=3, concat_axis=2, tiled=True)]
  transfers between devices with their start and end apart: 2 -> 2, of which waited for: 2 -> 2; matrix products, arithmetic and copies ran while one was open for 6% -> 1% of each run, Pallas kernels for 0% -> 0%
where the time goes in v1:
time: 179 us; the launch traced here: 177 us
  blocking collectives  59.5 us (33%)
  waiting for transfers between devices  50.8 us (28%)
  Pallas kernels  45.5 us (25%)
  starting transfers between devices  13.1 us (7%)
  local copies, waits for them, and re-layouts  8.29 us (5%)
    all_to_all x1, blocking collectives, body(): lax.all_to_all(cells, 'wide', split_axis=0, concat_axis=0, tiled=True)  45.1 us
    all_to_all x1, waiting for transfers between devices, body(): lax.all_to_all(rows, 'wide', split_axis=0, concat_axis=0, tiled=True)  43 us
    pallas_call x1, Pallas kernels, body(): pl.pallas_call(backward_cells, grid=(16,), in_specs=[pl.BlockSpec((C, 1,...  20.5 us
    all_to_all x1, blocking collectives, body(): lax.all_to_all(modes, 'narrow', split_axis=0, concat_axis=0, tiled=True)  14.5 us
    pallas_call x1, Pallas kernels, body(): pl.pallas_call(forward_cells, grid=(16,), in_specs=[pl.BlockSpec((C, 1, 3...  14 us
    unnamed x32, local copies, waits for them, and re-layouts  8.29 us
    all_to_all x1, waiting for transfers between devices, body(): lax.all_to_all(rows, 'narrow', split_axis=0, concat_axis=0, tiled=True)  7.79 us
    all_to_all x1, starting transfers between devices, body(): lax.all_to_all(rows, 'wide', split_axis=0, concat_axis=0, tiled=True)  7.39 us
  transfers between devices with their start and end apart: 2, of which 2 were waited for; matrix products, arithmetic and copies ran while one was open for 1% of the time, Pallas kernels for 0%

profile of v1, /device:TPU:17, one launch (start us, length us, event | category | flops | bytes accessed | tf_op | source)
XLA Modules:
  0.0 177.3 jit_solution(12321614566682551388)
XLA Ops:
  0.0 0.0 copy-start.6
  0.0 1.0 copy-done.6
  1.0 1.0 copy-done.7
  2.1 0.8 copy-done.8
  2.9 0.7 copy-done.11
  3.6 14.0 %forward_cells.1 = f32[16,96,512]{2,1,0:T(8,128)S(1)} custom-call(f32[20,16,32,256]{3,2,1,0:T(8,128)} %x_ref.3, bf16[128,256]{1,0:T(8,128)(2,1)S(1)} %copy-done.8, bf16[4,256,256]{2,1,0:T(8,128)(2,1)S(1)} %copy-done.7, bf16[4,256,256]{2,1,0:T(8,128)(2,1)S(1)} %copy-done.6, f32[8,2,128]{2,1,0:T(2,128)S(1)} %copy-done.11), custom_call_target="tpu_custom_call" | custom-call | tf_op jit(solution)/shard_map/forward_cells/pallas_call | solution.py:304
  17.6 0.0 copy-start.2
  17.6 0.0 copy-start.3
  17.6 45.1 %all_to_all.20.in_ref = f32[16,96,512]{2,1,0:T(8,128)S(1)} all-to-all(f32[16,96,512]{2,1,0:T(8,128)S(1)} %forward_cells.1), channel_id=1, replica_groups=mesh['wide'=16,'narrow'=8] {'wide'}, dimensions={0} | all-to-all | bytes 6291456 | tf_op jit(solution)/shard_map/all_to_all | solution.py:320
  62.7 0.0 copy-done.2
  62.7 0.0 copy-done.3
  62.7 4.1 %forward_rows.1 = f32[8,40,512]{2,1,0:T(8,128)} custom-call(bf16[320,1536]{1,0:T(8,128)(2,1)S(1)} %copy-done.3, bf16[320,1536]{1,0:T(8,128)(2,1)S(1)} %copy-done.2, f32[16,96,512]{2,1,0:T(8,128)S(1)} %all_to_all.20.in_ref), custom_call_target="tpu_custom_call" | custom-call | tf_op jit(solution)/shard_map/forward_rows/pallas_call | solution.py:324
  66.8 5.8 %all-to-all-start.1 = ((f32[8,40,512]{2,1,0:T(8,128)}), f32[8,40,512]{2,1,0:T(8,128)}, u32[]{:S(2)}, u32[]{:S(2)}) async-start(f32[8,40,512]{2,1,0:T(8,128)} %forward_rows.1), calls=%async_computation.1 | async-start | bytes 1310720 | tf_op jit(solution)/shard_map/all_to_all | solution.py:337
  72.5 2.5 %copy.21 = f32[1,2,20,20,3,144]{5,4,3,2,1,0:T(4,128)S(1)} copy(f32[1,2,20,20,3,144]{5,1,4,3,2,0:T(2,128)} %param.17) | data formatting | bytes 2764800 | tf_op args[1]
  75.1 7.8 %all-to-all-done.1.in_ref = f32[8,40,512]{2,1,0:T(8,128)} async-done(((f32[8,40,512]{2,1,0:T(8,128)}), f32[8,40,512]{2,1,0:T(8,128)}, u32[]{:S(2)}, u32[]{:S(2)}) %all-to-all-start.1) | async-done | bytes 655392 | tf_op jit(solution)/shard_map/all_to_all | solution.py:337
  82.9 2.8 %mix.1 = f32[8,40,512]{2,1,0:T(8,128)S(1)} custom-call(f32[8,40,512]{2,1,0:T(8,128)} %all-to-all-done.1.in_ref, f32[2,20,20,3,144]{4,3,2,1,0:T(4,128)S(1)} %bitcast.6), custom_call_target="tpu_custom_call" | custom-call | tf_op jit(solution)/shard_map/mix/pallas_call | solution.py:339
  85.7 14.5 %all_to_all.21.in_ref = f32[8,40,512]{2,1,0:T(8,128)S(1)} all-to-all(f32[8,40,512]{2,1,0:T(8,128)S(1)} %mix.1), channel_id=1, replica_groups=mesh['wide'=16,'narrow'=8] {'narrow'}, dimensions={0} | all-to-all | bytes 1310720 | tf_op jit(solution)/shard_map/all_to_all | solution.py:345
  100.1 0.0 copy-done
  100.2 0.0 copy-done.1
  100.2 4.1 %backward_rows.1 = f32[16,96,512]{2,1,0:T(8,128)} custom-call(bf16[1536,320]{1,0:T(8,128)(2,1)S(1)} %copy-done.1, bf16[1536,320]{1,0:T(8,128)(2,1)S(1)} %copy-done, f32[8,40,512]{2,1,0:T(8,128)S(1)} %all_to_all.21.in_ref), custom_call_target="tpu_custom_call" | custom-call | tf_op jit(solution)/shard_map/backward_rows/pallas_call | solution.py:347
  104.3 0.0 copy-start.13
  104.3 7.4 %all-to-all-start.3 = ((f32[16,96,512]{2,1,0:T(8,128)}), f32[16,96,512]{2,1,0:T(8,128)S(1)}, u32[]{:S(2)}, u32[]{:S(2)}) async-start(f32[16,96,512]{2,1,0:T(8,128)} %backward_rows.1), calls=%async_computation.3 | async-start | bytes 6291456 | tf_op jit(solution)/shard_map/all_to_all | solution.py:360
  111.7 0.0 copy-done.14
  111.7 43.0 %all-to-all-done.3.in_ref = f32[16,96,512]{2,1,0:T(8,128)S(1)} async-done(((f32[16,96,512]{2,1,0:T(8,128)}), f32[16,96,512]{2,1,0:T(8,128)S(1)}, u32[]{:S(2)}, u32[]{:S(2)}) %all-to-all-start.3) | async-done | bytes 3145760 | tf_op jit(solution)/shard_map/all_to_all | solution.py:360
  154.7 0.0 copy-done.9
  154.7 0.0 copy-done.10
  154.7 0.0 copy-done.12
  154.7 0.0 copy-done.13
  154.7 0.0 copy-start.4
  154.7 1.0 copy-done.4
  155.8 1.0 copy-done.5
  156.8 20.5 %backward_cells.1 = f32[20,16,32,256]{3,2,1,0:T(8,128)} custom-call(f32[20,16,32,256]{3,2,1,0:T(8,128)} %x_ref.3, f32[16,96,512]{2,1,0:T(8,128)S(1)} %all-to-all-done.3.in_ref, bf16[64,256]{1,0:T(8,128)(2,1)S(1)} %copy-done.10, bf16[64,256]{1,0:T(8,128)(2,1)S(1)} %copy-done.9, bf16[4,256,256]{2,1,0:T(8,128)(2,1)S(1)} %copy-done.5, ...), custom_call_target="tpu_custom_call" | custom-call | tf_op jit(solution)/shard_map/backward_cells/pallas_call | solution.py:367
  (11 shorter events, 0.0 us)
Async XLA Ops:
  0.0 1.0 copy-start.6
  1.0 1.0 copy-start.7
  2.1 0.8 copy-start.8
  2.9 0.7 copy-start.11
  17.6 45.1 %copy-start.2 = (bf16[320,1536]{1,0:T(8,128)(2,1)S(1)}, bf16[320,1536]{1,0:T(8,128)(2,1)}, u32[]{:S(2)}) copy-start(bf16[320,1536]{1,0:T(8,128)(2,1)} %constant.29.clone.low_ref) | copy-start | bytes 2949124
  17.6 45.1 %copy-start.3 = (bf16[320,1536]{1,0:T(8,128)(2,1)S(1)}, bf16[320,1536]{1,0:T(8,128)(2,1)}, u32[]{:S(2)}) copy-start(bf16[320,1536]{1,0:T(8,128)(2,1)} %constant.28.clone.high_ref) | copy-start | bytes 2949124
  66.8 16.1 %all-to-all-start.1 = ((f32[8,40,512]{2,1,0:T(8,128)}), f32[8,40,512]{2,1,0:T(8,128)}, u32[]{:S(2)}, u32[]{:S(2)}) async-start(f32[8,40,512]{2,1,0:T(8,128)} %forward_rows.1), calls=%async_computation.1 | async-start | bytes 1310720 | tf_op jit(solution)/shard_map/all_to_all | solution.py:337
  82.9 17.3 %copy-start = (bf16[1536,320]{1,0:T(8,128)(2,1)S(1)}, bf16[1536,320]{1,0:T(8,128)(2,1)}, u32[]{:S(2)}) copy-start(bf16[1536,320]{1,0:T(8,128)(2,1)} %constant.31.clone.low_ref) | copy-start | bytes 2949124
  82.9 17.3 %copy-start.1 = (bf16[1536,320]{1,0:T(8,128)(2,1)S(1)}, bf16[1536,320]{1,0:T(8,128)(2,1)}, u32[]{:S(2)}) copy-start(bf16[1536,320]{1,0:T(8,128)(2,1)} %constant.30.clone.high_ref) | copy-start | bytes 2949124
  104.3 7.4 %copy-start.14 = (f32[1,20,20]{2,0,1:T(1,128)S(1)}, f32[1,20,20]{2,0,1:T(1,128)}, u32[]{:S(2)}) copy-start(f32[1,20,20]{2,0,1:T(1,128)} %param.18) | copy-start | bytes 4804
  104.3 50.4 %copy-start.9 = (bf16[64,256]{1,0:T(8,128)(2,1)S(1)}, bf16[64,256]{1,0:T(8,128)(2,1)}, u32[]{:S(2)}) copy-start(bf16[64,256]{1,0:T(8,128)(2,1)} %constant.33.clone.el_ref) | copy-start | bytes 98308
  104.3 50.4 %copy-start.10 = (bf16[64,256]{1,0:T(8,128)(2,1)S(1)}, bf16[64,256]{1,0:T(8,128)(2,1)}, u32[]{:S(2)}) copy-start(bf16[64,256]{1,0:T(8,128)(2,1)} %constant.32.clone.eh_ref) | copy-start | bytes 98308
  104.3 50.4 %copy-start.12 = (f32[8,2,128]{2,1,0:T(2,128)S(1)}, f32[8,2,128]{2,1,0:T(2,128)}, u32[]{:S(2)}) copy-start(f32[8,2,128]{2,1,0:T(2,128)} %constant.27.clone.phase_ref) | copy-start | bytes 24580
  104.3 50.4 %copy-start.13 = (f32[1,20]{1,0:T(1,128)S(1)}, f32[1,20]{1,0:T(1,128)}, u32[]{:S(2)}) copy-start(f32[1,20]{1,0:T(1,128)} %bias_ref.1) | copy-start | bytes 244
  104.3 50.4 %all-to-all-start.3 = ((f32[16,96,512]{2,1,0:T(8,128)}), f32[16,96,512]{2,1,0:T(8,128)S(1)}, u32[]{:S(2)}, u32[]{:S(2)}) async-start(f32[16,96,512]{2,1,0:T(8,128)} %backward_rows.1), calls=%async_computation.3 | async-start | bytes 6291456 | tf_op jit(solution)/shard_map/all_to_all | solution.py:360
  154.7 1.0 copy-start.4
  155.8 1.0 copy-start.5

commit v2 on v1

v2 whole, which is shorter than its diff:
```python
import functools

import jax
import jax.numpy as jnp
import ml_dtypes
import numpy as np
from jax import lax
from jax.experimental import pallas as pl
from jax.experimental.pallas import tpu as pltpu
from jax.sharding import PartitionSpec as P

N = 256
C = 20
MX = 48
MY = 48
MZ = 24
WIDE = 16
NARROW = 8
HALF = 24
SEQS = 49
GROUPS = 4
LANES = GROUPS * 128
ROWS = 40

f32 = jnp.float32
bf16 = jnp.bfloat16


def signed(count):
    half = count // 2
    return np.concatenate([np.arange(half), np.arange(half) - half])


def halves(table):
    high = table.astype(ml_dtypes.bfloat16)
    low = (table - high.astype(np.float64)).astype(ml_dtypes.bfloat16)
    return high, low


def x_table():
    angle = 2 * np.pi * (np.outer(np.arange(HALF + 1), np.arange(N)) % N) / N
    table = np.zeros((64, N))
    table[: HALF + 1] = np.cos(angle)
    table[HALF + 1 : SEQS] = np.sin(angle[1:])
    return table


def z_table(scale):
    angle = 2 * np.pi * np.outer(np.arange(32), np.arange(MZ)) / N
    table = np.zeros((352, 256))
    for channel in range(5):
        rows = slice(96 + 32 * channel, 128 + 32 * channel)
        lanes = MZ * channel
        table[rows, lanes : lanes + MZ] = np.cos(angle) * scale
        table[rows, 128 + lanes : 128 + lanes + MZ] = np.sin(angle) * scale
    return table


def window_of(ref, group):
    return ref[96 - 32 * group : 352 - 32 * group]


def phase_table():
    angle = 2 * np.pi * (np.outer(np.arange(NARROW), np.arange(MZ)) % 8) / 8
    table = np.zeros((NARROW, 2, 128), np.float32)
    for channel in range(5):
        table[:, 0, MZ * channel : MZ * channel + MZ] = np.cos(angle)
        table[:, 1, MZ * channel : MZ * channel + MZ] = np.sin(angle)
    return table


def y_tables():
    angle = 2 * np.pi * (np.outer(signed(MY), np.arange(N)) % N) / N
    cosine = np.cos(angle).reshape(NARROW, 6, WIDE, 2, 8)
    sine = np.sin(angle).reshape(NARROW, 6, WIDE, 2, 8)
    forward = np.zeros((NARROW, ROWS, WIDE, 2, 3, 2, 8))
    backward = np.zeros((WIDE, 2, 3, 2, 8, NARROW, ROWS))
    for ky in range(6):
        for kx in range(3):
            real, imag = 6 * ky + kx, 6 * ky + 3 + kx
            c, s = cosine[:, ky], sine[:, ky]
            forward[:, real, :, :, kx, 0] = c
            forward[:, real, :, :, kx, 1] = s
            forward[:, imag, :, :, kx, 0] = -s
            forward[:, imag, :, :, kx, 1] = c
            c, s = (np.moveaxis(t, 0, -1) / N for t in (c, s))
            backward[:, :, kx, 0, :, :, real] = c
            backward[:, :, kx, 0, :, :, imag] = -s
            backward[:, :, kx, 1, :, :, real] = s
            backward[:, :, kx, 1, :, :, imag] = c
    return (
        forward.reshape(NARROW * ROWS, WIDE * 96),
        backward.reshape(WIDE * 96, NARROW * ROWS),
    )


def split(value):
    high = value.astype(bf16)
    return high, (value - high.astype(f32)).astype(bf16)


def dot(left, right, contract=((1,), (0,))):
    return lax.dot_general(left, right, (contract, ((), ())), preferred_element_type=f32)


def dot3(left, right, contract=((1,), (0,))):
    return (
        dot(left[0], right[0], contract)
        + dot(left[0], right[1], contract)
        + dot(left[1], right[0], contract)
    )


def forward_cells(
    x_ref, e_ref, zh_ref, zl_ref, phase_ref, out_ref, x_buf, out_buf, seq_ref, in_sem, out_sem
):
    def fetch(y):
        return pltpu.make_async_copy(x_ref.at[:, y], x_buf.at[y], in_sem.at[y])

    def leave(half):
        at = pl.ds(48 * half, 48)
        return pltpu.make_async_copy(out_buf.at[:, at], out_ref.at[:, at], out_sem.at[half])

    for y in range(16):
        fetch(y).start()

    def half_step(half, carry):
        def row_step(row, carry):
            y = 8 * half + row
            fetch(y).wait()
            high, low = split(x_buf[y].reshape(C * 32, N))
            both = dot(e_ref[...], high, ((1,), (1,)))
            seqs = both[:56] + both[64:120] + dot(e_ref[:64], low, ((1,), (1,)))[:56]
            for tile in range(5):
                seq_ref[tile, pl.ds(row, 56, stride=8), :] = seqs[:, 128 * tile : 128 * tile + 128]
            return carry

        lax.fori_loop(0, 8, row_step, 0)
        base = pl.multiple_of(48 * half, 8)
        turn = phase_ref[lax.axis_index("narrow")]
        turn_c, turn_s = turn[0:1], turn[1:2]
        for group in range(GROUPS):
            window = jnp.concatenate(
                [seq_ref[group, : SEQS * 8, :], seq_ref[group + 1, : SEQS * 8, :]], axis=1
            )
            modes = dot3(split(window), (window_of(zh_ref, group), window_of(zl_ref, group)))
            cosine, sine = modes[:, :128], modes[:, 128:]
            cosine, sine = turn_c * cosine - turn_s * sine, turn_s * cosine + turn_c * sine
            lanes = slice(128 * group, 128 * group + 128)
            for index in range(MX):
                freq = index if index < 24 else 48 - index
                at = slice(8 * freq, 8 * freq + 8)
                real, imag = cosine[at], -sine[at]
                if freq:
                    at = slice(8 * (24 + freq), 8 * (24 + freq) + 8)
                    if index < 24:
                        real, imag = real - sine[at], imag - cosine[at]
                    else:
                        real, imag = real + sine[at], imag + cosine[at]
                kx = 16 * (index % 3)
                out_buf[index // 3, pl.ds(base + kx, 8), lanes] = real
                out_buf[index // 3, pl.ds(base + kx + 8, 8), lanes] = imag
        leave(half).start()
        return carry

    lax.fori_loop(0, 2, half_step, 0)
    for half in range(2):
        leave(half).wait()


def forward_rows(high_ref, low_ref, in_ref, out_ref):
    part = dot3((high_ref[...], low_ref[...]), split(in_ref[...].reshape(-1, LANES)))
    out_ref[...] = part.reshape(NARROW, ROWS, LANES)


def mix(in_ref, w_ref, out_ref):
    total = jnp.sum(in_ref[...], axis=0)
    lane = lax.broadcasted_iota(jnp.int32, (8, 128), 1)
    rows = [total[6 * ky : 6 * ky + 8] for ky in range(5)]
    rows.append(jnp.concatenate([total[30:36], total[30:32]], axis=0))

    def roll(value, shift):
        shift = shift % 128
        return pltpu.roll(value, shift, 1) if shift else value

    spectra = []
    for channel in range(C):
        group, place = divmod(channel, 5)
        first = jnp.zeros((8, 128), f32)
        for ky in range(6):
            block = roll(rows[ky][:, 128 * group : 128 * group + 128], MZ * (ky - place))
            first = jnp.where(lane >= MZ * ky, block, first)
        spectra.append(jnp.concatenate([first, block], axis=1)[:, :144])
    mixed = []
    for start in range(0, C, 5):
        real = jnp.zeros((5, 3, 144), f32)
        imag = jnp.zeros((5, 3, 144), f32)
        for channel in range(C):
            a, b = spectra[channel][None, 0:3], spectra[channel][None, 3:6]
            u = w_ref[0, channel, start : start + 5]
            v = w_ref[1, channel, start : start + 5]
            real += a * u - b * v
            imag += a * v + b * u
        for place in range(5):
            mixed.append(jnp.concatenate([real[place], imag[place]], axis=0))
    lane = lane[:6]
    for group in range(GROUPS):
        for ky in range(6):
            tile = jnp.zeros((6, 128), f32)
            for place in range(5):
                value = mixed[5 * group + place]
                block = value[:, :128]
                if ky == 5:
                    rest = jnp.concatenate([value[:, 128:], jnp.zeros((6, 112), f32)], axis=1)
                    block = jnp.where(lane >= 120, block, rest)
                block = roll(block, MZ * (place - ky))
                inside = (lane >= MZ * place) & (lane < MZ * place + MZ)
                tile = jnp.where(inside, block, tile)
            for narrow in range(NARROW):
                out_ref[narrow, 6 * ky : 6 * ky + 6, 128 * group : 128 * group + 128] = tile
    for narrow in range(NARROW):
        out_ref[narrow, 36:40, :] = jnp.zeros((4, LANES), f32)


def backward_rows(table_ref, in_ref, out_ref):
    high, low = split(in_ref[...].reshape(-1, LANES))
    part = dot(table_ref[...], jnp.concatenate([high, low, high], axis=0))
    out_ref[...] = part.reshape(out_ref.shape)


def gelu(value):
    return 0.5 * value * (1.0 + lax.erf(value * np.float32(np.sqrt(0.5))))


def linear_cells(
    x_ref, lin_ref, bias_ref, out_ref, x_buf, out_buf, lh_ref, ll_ref, in_sem, out_sem
):
    def fetch(y):
        return pltpu.make_async_copy(x_ref.at[:, y], x_buf.at[y], in_sem.at[y])

    def leave(y):
        return pltpu.make_async_copy(out_buf.at[y], out_ref.at[:, y], out_sem.at[y])

    for y in range(16):
        fetch(y).start()
    spread = lax.broadcasted_iota(jnp.int32, (160, C), 0) // 8
    spread = (spread == lax.broadcasted_iota(jnp.int32, (160, C), 1)).astype(bf16)
    rows = lax.broadcasted_iota(jnp.int32, (160, 160), 0)
    cols = lax.broadcasted_iota(jnp.int32, (160, 160), 1)
    same = (rows & 7) == (cols & 7)
    for part, ref in zip(split(lin_ref[...]), (lh_ref, ll_ref)):
        wide = dot(spread, part, ((1,), (1,))).astype(bf16)
        wide = dot(wide, spread, ((1,), (1,)))
        ref[...] = jnp.where(same, wide, 0.0).astype(bf16)

    def row_step(y, carry):
        fetch(y).wait()
        for block in range(4):
            at = slice(8 * block, 8 * block + 8)
            cells = split(x_buf[y, :, at, :].reshape(C * 8, N))
            linear = dot3((lh_ref[...], ll_ref[...]), cells).reshape(C, 8, N)
            for channel in range(C):
                out_buf[y, channel, at, :] = linear[channel] + bias_ref[0, channel]
        leave(y).start()
        return carry

    lax.fori_loop(0, 16, row_step, 0)
    for y in range(16):
        leave(y).wait()


def backward_cells(
    linear_ref, in_ref, e_ref, zh_ref, zl_ref, phase_ref, out_ref,
    x_buf, in_buf, out_buf, cell_ref, x_sem, in_sem, out_sem,
):
    def modes_in(half):
        at = pl.ds(48 * half, 48)
        return pltpu.make_async_copy(in_ref.at[:, at], in_buf.at[:, at], in_sem.at[half])

    def fetch(y):
        return pltpu.make_async_copy(linear_ref.at[:, y], x_buf.at[y], x_sem.at[y])

    def leave(y):
        return pltpu.make_async_copy(out_buf.at[y], out_ref.at[:, y], out_sem.at[y])

    for half in range(2):
        modes_in(half).start()
    for y in range(16):
        fetch(y).start()
    for tile in range(5):
        cell_ref[tile, SEQS * 8 :, :] = jnp.zeros((512 - SEQS * 8, 128), f32)

    def half_step(half, carry):
        modes_in(half).wait()
        base = 48 * half
        turn = phase_ref[lax.axis_index("narrow")]
        turn_c, turn_s = turn[0:1], turn[1:2]
        last = None
        for group in range(GROUPS):
            lanes = slice(128 * group, 128 * group + 128)

            def mode(index, part):
                at = base + 16 * (index % 3) + 8 * part
                return in_buf[index // 3, pl.ds(pl.multiple_of(at, 8), 8), lanes]

            first, second = [], []
            for freq in range(HALF + 1):
                if freq == 0:
                    u, v = mode(0, 0), mode(0, 1)
                elif freq == HALF:
                    u, v = mode(48 - freq, 0), mode(48 - freq, 1)
                else:
                    u = mode(freq, 0) + mode(48 - freq, 0)
                    v = mode(freq, 1) + mode(48 - freq, 1)
                first.append(u)
                second.append(v)
            for freq in range(1, HALF + 1):
                if freq == HALF:
                    u, v = mode(48 - freq, 1), -mode(48 - freq, 0)
                else:
                    u = mode(48 - freq, 1) - mode(freq, 1)
                    v = mode(freq, 0) - mode(48 - freq, 0)
                first.append(u)
                second.append(v)
            u, v = jnp.concatenate(first, axis=0), jnp.concatenate(second, axis=0)
            u, v = turn_c * u - turn_s * v, turn_s * u + turn_c * v
            cells = dot3(
                split(jnp.concatenate([u, v], axis=1)),
                (window_of(zh_ref, group), window_of(zl_ref, group)),
                ((1,), (1,)),
            )
            left, right = cells[:, :128], cells[:, 128:]
            cell_ref[group, : SEQS * 8, :] = left if last is None else left + last
            last = right
        cell_ref[GROUPS, : SEQS * 8, :] = last

        def row_step(row, carry):
            y = 8 * half + row
            seqs = jnp.concatenate(
                [cell_ref[tile, pl.ds(row, 64, stride=8), :] for tile in range(5)], axis=1
            )
            pair = jnp.transpose(jnp.concatenate(split(seqs), axis=0))
            spatial = dot(jnp.concatenate([pair, pair], axis=1), e_ref[...])
            fetch(y).wait()
            out_buf[y] = gelu(x_buf[y] + spatial.reshape(C, 32, N))
            leave(y).start()
            return carry

        lax.fori_loop(0, 8, row_step, 0)
        return carry

    lax.fori_loop(0, 2, half_step, 0)
    for y in range(16):
        leave(y).wait()


def whole(shape):
    return pl.BlockSpec(shape, lambda *_: (0,) * len(shape))


def params(mib):
    return pltpu.CompilerParams(
        dimension_semantics=("arbitrary",), vmem_limit_bytes=mib * 1024 * 1024
    )


def cells_forward(field):
    eh, el = halves(x_table())
    zh, zl = halves(z_table(1.0))
    vmem = pl.BlockSpec(memory_space=pltpu.VMEM)
    return pl.pallas_call(
        forward_cells,
        in_specs=[pl.BlockSpec(memory_space=pl.ANY), vmem, vmem, vmem, vmem],
        out_specs=pl.BlockSpec(memory_space=pl.ANY),
        out_shape=jax.ShapeDtypeStruct((WIDE, 96, LANES), f32),
        scratch_shapes=[
            pltpu.VMEM((16, C, 32, N), f32),
            pltpu.VMEM((WIDE, 96, LANES), f32),
            pltpu.VMEM((5, 512, 128), f32),
            pltpu.SemaphoreType.DMA((16,)),
            pltpu.SemaphoreType.DMA((2,)),
        ],
        compiler_params=pltpu.CompilerParams(vmem_limit_bytes=60 * 1024 * 1024),
        name="forward_cells",
    )(
        field,
        np.concatenate([eh, el]),
        zh,
        zl,
        phase_table(),
    )


def rows_forward(moved):
    high, low = halves(y_tables()[0])
    return pl.pallas_call(
        forward_rows,
        out_shape=jax.ShapeDtypeStruct((NARROW, ROWS, LANES), f32),
        compiler_params=pltpu.CompilerParams(vmem_limit_bytes=32 * 1024 * 1024),
        name="forward_rows",
    )(high, low, moved)


def mix_modes(moved, spec_weight):
    return pl.pallas_call(
        mix,
        out_shape=jax.ShapeDtypeStruct((NARROW, ROWS, LANES), f32),
        compiler_params=pltpu.CompilerParams(vmem_limit_bytes=32 * 1024 * 1024),
        name="mix",
    )(moved, spec_weight.reshape(2, C, C, 3, 144))


def rows_backward(moved):
    high, low = halves(y_tables()[1])
    return pl.pallas_call(
        backward_rows,
        grid=(2,),
        in_specs=[
            pl.BlockSpec((768, 3 * NARROW * ROWS), lambda s: (s, 0)),
            whole((NARROW, ROWS, LANES)),
        ],
        out_specs=pl.BlockSpec((8, 96, LANES), lambda s: (s, 0, 0)),
        out_shape=jax.ShapeDtypeStruct((WIDE, 96, LANES), f32),
        compiler_params=params(32),
        name="backward_rows",
    )(np.concatenate([high, high, low], axis=1), moved)


def linear_part(field, lin_weight, bias):
    return pl.pallas_call(
        linear_cells,
        in_specs=[
            pl.BlockSpec(memory_space=pl.ANY),
            pl.BlockSpec(memory_space=pltpu.VMEM),
            pl.BlockSpec(memory_space=pltpu.SMEM),
        ],
        out_specs=pl.BlockSpec(memory_space=pl.ANY),
        out_shape=jax.ShapeDtypeStruct(field.shape, f32),
        scratch_shapes=[
            pltpu.VMEM((16, C, 32, N), f32),
            pltpu.VMEM((16, C, 32, N), f32),
            pltpu.VMEM((160, 160), bf16),
            pltpu.VMEM((160, 160), bf16),
            pltpu.SemaphoreType.DMA((16,)),
            pltpu.SemaphoreType.DMA((16,)),
        ],
        compiler_params=pltpu.CompilerParams(vmem_limit_bytes=40 * 1024 * 1024),
        cost_estimate=pl.CostEstimate(
            flops=2 * 3 * 160 * field.size, bytes_accessed=8 * field.size, transcendentals=0
        ),
        name="linear_cells",
    )(field, lin_weight.reshape(C, C), bias)


def cells_backward(linear, moved):
    eh, el = halves(x_table() / N)
    scale = np.where(np.arange(MZ) == 0, 1.0, 2.0) / N
    table = z_table(scale)
    table[:, 128:] *= -1
    zh, zl = halves(table)
    vmem = pl.BlockSpec(memory_space=pltpu.VMEM)
    hbm = pl.BlockSpec(memory_space=pl.ANY)
    return pl.pallas_call(
        backward_cells,
        in_specs=[hbm, hbm, vmem, vmem, vmem, vmem],
        out_specs=hbm,
        out_shape=jax.ShapeDtypeStruct(linear.shape, f32),
        scratch_shapes=[
            pltpu.VMEM((16, C, 32, N), f32),
            pltpu.VMEM((WIDE, 96, LANES), f32),
            pltpu.VMEM((16, C, 32, N), f32),
            pltpu.VMEM((5, 512, 128), f32),
            pltpu.SemaphoreType.DMA((16,)),
            pltpu.SemaphoreType.DMA((2,)),
            pltpu.SemaphoreType.DMA((16,)),
        ],
        compiler_params=pltpu.CompilerParams(vmem_limit_bytes=60 * 1024 * 1024),
        name="backward_cells",
    )(linear, moved, np.concatenate([eh, eh, el, np.zeros_like(el)]), zh, zl, phase_table())


def body(field, spec_weight, lin_weight, bias):
    moved = cells_forward(field)
    moved = lax.all_to_all(moved, "wide", split_axis=0, concat_axis=0, tiled=True)
    moved = rows_forward(moved)
    moved = lax.all_to_all(moved, "narrow", split_axis=0, concat_axis=0, tiled=True)
    moved = mix_modes(moved, spec_weight)
    moved = lax.all_to_all(moved, "narrow", split_axis=0, concat_axis=0, tiled=True)
    moved = rows_backward(moved)
    moved = lax.all_to_all(moved, "wide", split_axis=0, concat_axis=0, tiled=True)
    linear = linear_part(field, lin_weight, bias)
    return cells_backward(linear, moved)


def solution(mesh):
    placed = (
        P(None, "wide", "narrow", None),
        P(None, None, None, None, "wide", "narrow"),
        P(),
        P(),
    )
    return jax.shard_map(
        body, mesh=mesh, in_specs=placed, out_specs=P(None, "wide", "narrow", None), check_vma=False
    )
```

time: 179 us -> 162 us (0.905)
  waiting for transfers between devices: 50.8 us -> 37.2 us
  Pallas kernels: 45.5 us -> 43.6 us
    all_to_all x2, waiting for transfers between devices: 50.8 us -> 37.2 us  [the longest x1 29.4 us: body(): lax.all_to_all(moved, 'wide', split_axis=0, concat_axis=0, tiled=True)]
    pallas_call x5 -> x6, Pallas kernels: 45.5 us -> 43.6 us  [the longest x1 15 us: cells_backward(): pl.pallas_call(backward_cells, in_specs=[hbm, hbm, vmem, vmem, vmem, vmem...]
    unnamed x32 -> x16, local copies, waits for them, and re-layouts: 8.29 us -> 8.29 us
  transfers between devices with their start and end apart: 2 -> 2, of which waited for: 2 -> 2; matrix products, arithmetic and copies ran while one was open for 1% -> 2% of each run, Pallas kernels for 0% -> 6%
where the time goes in v2:
time: 162 us
  blocking collectives  59.7 us (37%)
  Pallas kernels  43.6 us (27%)
  waiting for transfers between devices  37.2 us (23%)
  starting transfers between devices  13.1 us (8%)
  local copies, waits for them, and re-layouts  8.29 us (5%)
    all_to_all x1, blocking collectives, body(): lax.all_to_all(moved, 'wide', split_axis=0, concat_axis=0, tiled=True)  45.3 us
    all_to_all x1, waiting for transfers between devices, body(): lax.all_to_all(moved, 'wide', split_axis=0, concat_axis=0, tiled=True)  29.4 us
    pallas_call x1, Pallas kernels, cells_backward(): pl.pallas_call(backward_cells, in_specs=[hbm, hbm, vmem, vmem, vmem, vmem...  15 us
    all_to_all x1, blocking collectives, body(): lax.all_to_all(moved, 'narrow', split_axis=0, concat_axis=0, tiled=True)  14.4 us
    pallas_call x1, Pallas kernels, cells_forward(): pl.pallas_call(forward_cells, in_specs=[pl.BlockSpec(memory_space=pl.ANY)...  10.5 us
    pallas_call x1, Pallas kernels, linear_part(): pl.pallas_call(linear_cells, in_specs=[pl.BlockSpec(memory_space=pl.ANY),...  9.61 us
    unnamed x16, local copies, waits for them, and re-layouts  8.29 us
    all_to_all x1, waiting for transfers between devices, body(): lax.all_to_all(moved, 'narrow', split_axis=0, concat_axis=0, tiled=True)  7.79 us
  transfers between devices with their start and end apart: 2, of which 2 were waited for; matrix products, arithmetic and copies ran while one was open for 2% of the time, Pallas kernels for 6%

profile of v2, /device:TPU:17, one launch (start us, length us, event | category | flops | bytes accessed | tf_op | source)
XLA Modules:
  0.0 162.0 jit_solution(4743745050861881772)
XLA Ops:
  0.0 10.5 %forward_cells.1 = f32[16,96,512]{2,1,0:T(8,128)} custom-call(f32[20,16,32,256]{3,2,1,0:T(8,128)} %x_ref.3, bf16[128,256]{1,0:T(8,128)(2,1)} %constant.20.clone.e_ref, bf16[352,256]{1,0:T(8,128)(2,1)} %constant.21.clone.zh_ref, bf16[352,256]{1,0:T(8,128)(2,1)} %constant.22.clone.zl_ref, f32[8,2,128]{2,1,0:T(2,128)} %constant.23.clone.phase_ref), custom_call_target="tpu_custom_call" | custom-call | tf_op jit(solution)/shard_map/forward_cells/pallas_call | solution.py:371
  10.5 0.0 copy-start.2
  10.5 0.0 copy-start.3
  10.5 45.3 %all_to_all.20.in_ref = f32[16,96,512]{2,1,0:T(8,128)S(1)} all-to-all(f32[16,96,512]{2,1,0:T(8,128)} %forward_cells.1), channel_id=1, replica_groups=mesh['wide'=16,'narrow'=8] {'wide'}, dimensions={0} | all-to-all | bytes 6291456 | tf_op jit(solution)/shard_map/all_to_all | solution.py:484
  55.8 0.0 copy-done.2
  55.8 0.0 copy-done.3
  55.8 2.6 %forward_rows.1 = f32[8,40,512]{2,1,0:T(8,128)} custom-call(bf16[320,1536]{1,0:T(8,128)(2,1)S(1)} %copy-done.3, bf16[320,1536]{1,0:T(8,128)(2,1)S(1)} %copy-done.2, f32[16,96,512]{2,1,0:T(8,128)S(1)} %all_to_all.20.in_ref), custom_call_target="tpu_custom_call" | custom-call | tf_op jit(solution)/shard_map/forward_rows/pallas_call | solution.py:396
  58.4 5.8 %all-to-all-start.1 = ((f32[8,40,512]{2,1,0:T(8,128)}), f32[8,40,512]{2,1,0:T(8,128)}, u32[]{:S(2)}, u32[]{:S(2)}) async-start(f32[8,40,512]{2,1,0:T(8,128)} %forward_rows.1), calls=%async_computation.1 | async-start | bytes 1310720 | tf_op jit(solution)/shard_map/all_to_all | solution.py:486
  64.1 2.5 %copy.20 = f32[1,2,20,20,3,144]{5,4,3,2,1,0:T(4,128)S(1)} copy(f32[1,2,20,20,3,144]{5,1,4,3,2,0:T(2,128)} %param.16) | data formatting | bytes 2764800 | tf_op args[1]
  66.7 7.8 %all-to-all-done.1.in_ref = f32[8,40,512]{2,1,0:T(8,128)} async-done(((f32[8,40,512]{2,1,0:T(8,128)}), f32[8,40,512]{2,1,0:T(8,128)}, u32[]{:S(2)}, u32[]{:S(2)}) %all-to-all-start.1) | async-done | bytes 655392 | tf_op jit(solution)/shard_map/all_to_all | solution.py:486
  74.5 0.0 copy-start.1
  74.5 2.8 %mix.1 = f32[8,40,512]{2,1,0:T(8,128)S(1)} custom-call(f32[8,40,512]{2,1,0:T(8,128)} %all-to-all-done.1.in_ref, f32[2,20,20,3,144]{4,3,2,1,0:T(4,128)S(1)} %bitcast.6), custom_call_target="tpu_custom_call" | custom-call | tf_op jit(solution)/shard_map/mix/pallas_call | solution.py:405
  77.3 14.4 %all_to_all.21.in_ref = f32[8,40,512]{2,1,0:T(8,128)S(1)} all-to-all(f32[8,40,512]{2,1,0:T(8,128)S(1)} %mix.1), channel_id=1, replica_groups=mesh['wide'=16,'narrow'=8] {'narrow'}, dimensions={0} | all-to-all | bytes 1310720 | tf_op jit(solution)/shard_map/all_to_all | solution.py:488
  91.8 0.0 copy-done.1
  91.8 3.1 %backward_rows.1 = f32[16,96,512]{2,1,0:T(8,128)} custom-call(bf16[1536,960]{1,0:T(8,128)(2,1)S(1)} %copy-done.1, f32[8,40,512]{2,1,0:T(8,128)S(1)} %all_to_all.21.in_ref), custom_call_target="tpu_custom_call" | custom-call | tf_op jit(solution)/shard_map/backward_rows/pallas_call | solution.py:415
  94.9 0.0 copy-start.6
  94.9 0.0 copy-start.4
  94.9 7.4 %all-to-all-start.3 = ((f32[16,96,512]{2,1,0:T(8,128)}), f32[16,96,512]{2,1,0:T(8,128)S(1)}, u32[]{:S(2)}, u32[]{:S(2)}) async-start(f32[16,96,512]{2,1,0:T(8,128)} %backward_rows.1), calls=%async_computation.3 | async-start | bytes 6291456 | tf_op jit(solution)/shard_map/all_to_all | solution.py:490
  102.2 0.0 copy-done.6
  102.3 0.0 copy-done.4
  102.3 9.6 %linear_cells.1.linear_ref = f32[20,16,32,256]{3,2,1,0:T(8,128)S(1)} custom-call(f32[20,16,32,256]{3,2,1,0:T(8,128)} %x_ref.3, f32[20,20]{1,0:T(8,128)S(1)} %bitcast.7, f32[1,20]{1,0:T(1,128)S(1)} %copy-done.4), custom_call_target="tpu_custom_call" | custom-call | flops 2516582400 | bytes 20971520 | tf_op jit(solution)/shard_map/linear_cells/pallas_call | solution.py:430
  111.9 0.0 copy-start
  111.9 4.0 %copy-done = f32[20,16,32,256]{3,2,1,0:T(8,128)} copy-done((f32[20,16,32,256]{3,2,1,0:T(8,128)}, f32[20,16,32,256]{3,2,1,0:T(8,128)S(1)}, u32[]{:S(2)}) %copy-start) | copy-done | bytes 10485784
  115.9 29.4 %all-to-all-done.3.in_ref = f32[16,96,512]{2,1,0:T(8,128)S(1)} async-done(((f32[16,96,512]{2,1,0:T(8,128)}), f32[16,96,512]{2,1,0:T(8,128)S(1)}, u32[]{:S(2)}, u32[]{:S(2)}) %all-to-all-start.3) | async-done | bytes 3145760 | tf_op jit(solution)/shard_map/all_to_all | solution.py:490
  145.2 0.0 copy-start.5
  145.2 1.8 %copy-done.5 = f32[16,96,512]{2,1,0:T(8,128)} copy-done((f32[16,96,512]{2,1,0:T(8,128)}, f32[16,96,512]{2,1,0:T(8,128)S(1)}, u32[]{:S(2)}) %copy-start.5) | copy-done | bytes 3145752
  147.0 15.0 %backward_cells.1 = f32[20,16,32,256]{3,2,1,0:T(8,128)} custom-call(f32[20,16,32,256]{3,2,1,0:T(8,128)} %copy-done, f32[16,96,512]{2,1,0:T(8,128)} %copy-done.5, bf16[256,256]{1,0:T(8,128)(2,1)} %constant.27.clone.e_ref, bf16[352,256]{1,0:T(8,128)(2,1)} %constant.28.clone.zh_ref, bf16[352,256]{1,0:T(8,128)(2,1)} %constant.29.clone.zl_ref, ...), custom_call_target="tpu_custom_call" | custom-call | tf_op jit(solution)/shard_map/backward_cells/pallas_call | solution.py:463
  (1 shorter events, 0.0 us)
Async XLA Ops:
  10.5 45.3 %copy-start.2 = (bf16[320,1536]{1,0:T(8,128)(2,1)S(1)}, bf16[320,1536]{1,0:T(8,128)(2,1)}, u32[]{:S(2)}) copy-start(bf16[320,1536]{1,0:T(8,128)(2,1)} %constant.25.clone.low_ref) | copy-start | bytes 2949124
  10.5 45.3 %copy-start.3 = (bf16[320,1536]{1,0:T(8,128)(2,1)S(1)}, bf16[320,1536]{1,0:T(8,128)(2,1)}, u32[]{:S(2)}) copy-start(bf16[320,1536]{1,0:T(8,128)(2,1)} %constant.24.clone.high_ref) | copy-start | bytes 2949124
  58.4 16.1 %all-to-all-start.1 = ((f32[8,40,512]{2,1,0:T(8,128)}), f32[8,40,512]{2,1,0:T(8,128)}, u32[]{:S(2)}, u32[]{:S(2)}) async-start(f32[8,40,512]{2,1,0:T(8,128)} %forward_rows.1), calls=%async_computation.1 | async-start | bytes 1310720 | tf_op jit(solution)/shard_map/all_to_all | solution.py:486
  74.5 17.3 %copy-start.1 = (bf16[1536,960]{1,0:T(8,128)(2,1)S(1)}, bf16[1536,960]{1,0:T(8,128)(2,1)}, u32[]{:S(2)}) copy-start(bf16[1536,960]{1,0:T(8,128)(2,1)} %constant.26.clone.table_ref) | copy-start | bytes 8847364
  94.9 7.4 %copy-start.6 = (f32[1,20,20]{2,0,1:T(1,128)S(1)}, f32[1,20,20]{2,0,1:T(1,128)}, u32[]{:S(2)}) copy-start(f32[1,20,20]{2,0,1:T(1,128)} %param.17) | copy-start | bytes 4804
  94.9 7.4 %copy-start.4 = (f32[1,20]{1,0:T(1,128)S(1)}, f32[1,20]{1,0:T(1,128)}, u32[]{:S(2)}) copy-start(f32[1,20]{1,0:T(1,128)} %bias_ref.1) | copy-start | bytes 244
  94.9 50.4 %all-to-all-start.3 = ((f32[16,96,512]{2,1,0:T(8,128)}), f32[16,96,512]{2,1,0:T(8,128)S(1)}, u32[]{:S(2)}, u32[]{:S(2)}) async-start(f32[16,96,512]{2,1,0:T(8,128)} %backward_rows.1), calls=%async_computation.3 | async-start | bytes 6291456 | tf_op jit(solution)/shard_map/all_to_all | solution.py:490
  111.9 4.0 %copy-start = (f32[20,16,32,256]{3,2,1,0:T(8,128)}, f32[20,16,32,256]{3,2,1,0:T(8,128)S(1)}, u32[]{:S(2)}) copy-start(f32[20,16,32,256]{3,2,1,0:T(8,128)S(1)} %linear_cells.1.linear_ref) | copy-start | bytes 31457284
  145.2 1.8 %copy-start.5 = (f32[16,96,512]{2,1,0:T(8,128)}, f32[16,96,512]{2,1,0:T(8,128)S(1)}, u32[]{:S(2)}) copy-start(f32[16,96,512]{2,1,0:T(8,128)S(1)} %all-to-all-done.3.in_ref) | copy-start | bytes 9437188

commit v3 on v2

--- a/solution.py
+++ b/solution.py
@@ -20,6 +20,7 @@
 SEQS = 49
 GROUPS = 4
 LANES = GROUPS * 128
+AHEAD = 6
 ROWS = 40
 
 f32 = jnp.float32
@@ -121,13 +122,18 @@
         at = pl.ds(48 * half, 48)
         return pltpu.make_async_copy(out_buf.at[:, at], out_ref.at[:, at], out_sem.at[half])
 
-    for y in range(16):
+    for y in range(AHEAD):
         fetch(y).start()
 
     def half_step(half, carry):
         def row_step(row, carry):
             y = 8 * half + row
             fetch(y).wait()
+
+            @pl.when(y + AHEAD < 16)
+            def _():
+                fetch(y + AHEAD).start()
+
             high, low = split(x_buf[y].reshape(C * 32, N))
             both = dot(e_ref[...], high, ((1,), (1,)))
             seqs = both[:56] + both[64:120] + dot(e_ref[:64], low, ((1,), (1,)))[:56]
@@ -173,6 +179,12 @@
     out_ref[...] = part.reshape(NARROW, ROWS, LANES)
 
 
+def arrange(w_ref, out_ref):
+    out_ref[...] = jnp.zeros(out_ref.shape, f32)
+    out_ref[:, :, 0:3, 0:144] = w_ref[0]
+    out_ref[:, :, 3:6, 0:144] = w_ref[1]
+
+
 def mix(in_ref, w_ref, out_ref):
     total = jnp.sum(in_ref[...], axis=0)
     lane = lax.broadcasted_iota(jnp.int32, (8, 128), 1)
@@ -190,19 +202,26 @@
         for ky in range(6):
             block = roll(rows[ky][:, 128 * group : 128 * group + 128], MZ * (ky - place))
             first = jnp.where(lane >= MZ * ky, block, first)
-        spectra.append(jnp.concatenate([first, block], axis=1)[:, :144])
+        value = jnp.concatenate([first, block], axis=1)
+        real, imag = value[0:3], value[3:6]
+        spectra.append(
+            (
+                jnp.concatenate([real, real, real[0:2]], axis=0)[None],
+                jnp.concatenate([imag, imag, imag[0:2]], axis=0)[None],
+            )
+        )
     mixed = []
     for start in range(0, C, 5):
-        real = jnp.zeros((5, 3, 144), f32)
-        imag = jnp.zeros((5, 3, 144), f32)
+        by_real = jnp.zeros((5, 8, 256), f32)
+        by_imag = jnp.zeros((5, 8, 256), f32)
         for channel in range(C):
-            a, b = spectra[channel][None, 0:3], spectra[channel][None, 3:6]
-            u = w_ref[0, channel, start : start + 5]
-            v = w_ref[1, channel, start : start + 5]
-            real += a * u - b * v
-            imag += a * v + b * u
+            weight = w_ref[channel, start : start + 5]
+            by_real += spectra[channel][0] * weight
+            by_imag += spectra[channel][1] * weight
         for place in range(5):
-            mixed.append(jnp.concatenate([real[place], imag[place]], axis=0))
+            real = by_real[place, 0:3] - by_imag[place, 3:6]
+            imag = by_real[place, 3:6] + by_imag[place, 0:3]
+            mixed.append(jnp.concatenate([real, imag], axis=0))
     lane = lane[:6]
     for group in range(GROUPS):
         for ky in range(6):
@@ -211,7 +230,7 @@
                 value = mixed[5 * group + place]
                 block = value[:, :128]
                 if ky == 5:
-                    rest = jnp.concatenate([value[:, 128:], jnp.zeros((6, 112), f32)], axis=1)
+                    rest = value[:, 128:]
                     block = jnp.where(lane >= 120, block, rest)
                 block = roll(block, MZ * (place - ky))
                 inside = (lane >= MZ * place) & (lane < MZ * place + MZ)
@@ -283,15 +302,19 @@
     def leave(y):
         return pltpu.make_async_copy(out_buf.at[y], out_ref.at[:, y], out_sem.at[y])
 
-    for half in range(2):
-        modes_in(half).start()
-    for y in range(16):
-        fetch(y).start()
+    modes_in(0).start()
     for tile in range(5):
         cell_ref[tile, SEQS * 8 :, :] = jnp.zeros((512 - SEQS * 8, 128), f32)
 
     def half_step(half, carry):
         modes_in(half).wait()
+
+        @pl.when(half == 0)
+        def _():
+            for y in range(AHEAD):
+                fetch(y).start()
+            modes_in(1).start()
+
         base = 48 * half
         turn = phase_ref[lax.axis_index("narrow")]
         turn_c, turn_s = turn[0:1], turn[1:2]
@@ -342,6 +365,11 @@
             pair = jnp.transpose(jnp.concatenate(split(seqs), axis=0))
             spatial = dot(jnp.concatenate([pair, pair], axis=1), e_ref[...])
             fetch(y).wait()
+
+            @pl.when(y + AHEAD < 16)
+            def _():
+                fetch(y + AHEAD).start()
+
             out_buf[y] = gelu(x_buf[y] + spatial.reshape(C, 32, N))
             leave(y).start()
             return carry
@@ -401,13 +429,25 @@
     )(high, low, moved)
 
 
-def mix_modes(moved, spec_weight):
+def arrange_weights(spec_weight):
+    return pl.pallas_call(
+        arrange,
+        grid=(4,),
+        in_specs=[pl.BlockSpec((2, 5, C, 3, 144), lambda i: (0, i, 0, 0, 0))],
+        out_specs=pl.BlockSpec((5, C, 8, 256), lambda i: (i, 0, 0, 0)),
+        out_shape=jax.ShapeDtypeStruct((C, C, 8, 256), f32),
+        compiler_params=params(32),
+        name="arrange",
+    )(spec_weight.reshape(2, C, C, 3, 144))
+
+
+def mix_modes(moved, weights):
     return pl.pallas_call(
         mix,
         out_shape=jax.ShapeDtypeStruct((NARROW, ROWS, LANES), f32),
         compiler_params=pltpu.CompilerParams(vmem_limit_bytes=32 * 1024 * 1024),
         name="mix",
-    )(moved, spec_weight.reshape(2, C, C, 3, 144))
+    )(moved, weights)
 
 
 def rows_backward(moved):
@@ -474,7 +514,7 @@
             pltpu.SemaphoreType.DMA((2,)),
             pltpu.SemaphoreType.DMA((16,)),
         ],
-        compiler_params=pltpu.CompilerParams(vmem_limit_bytes=60 * 1024 * 1024),
+        compiler_params=pltpu.CompilerParams(vmem_limit_bytes=46 * 1024 * 1024),
         name="backward_cells",
     )(linear, moved, np.concatenate([eh, eh, el, np.zeros_like(el)]), zh, zl, phase_table())
 
@@ -484,7 +524,7 @@
     moved = lax.all_to_all(moved, "wide", split_axis=0, concat_axis=0, tiled=True)
     moved = rows_forward(moved)
     moved = lax.all_to_all(moved, "narrow", split_axis=0, concat_axis=0, tiled=True)
-    moved = mix_modes(moved, spec_weight)
+    moved = mix_modes(moved, arrange_weights(spec_weight))
     moved = lax.all_to_all(moved, "narrow", split_axis=0, concat_axis=0, tiled=True)
     moved = rows_backward(moved)
     moved = lax.all_to_all(moved, "wide", split_axis=0, concat_axis=0, tiled=True)

time: 162 us -> 156 us (0.963)
  Pallas kernels: 43.6 us -> 38.8 us
  local copies, waits for them, and re-layouts: 8.29 us -> 5.79 us
    pallas_call x1, Pallas kernels: 15 us -> 10.1 us  [cells_backward(): pl.pallas_call(backward_cells, in_specs=[hbm, hbm, vmem, vmem, vmem, vmem...]
    unnamed x16 -> x24, local copies, waits for them, and re-layouts: 8.29 us -> 5.79 us
  transfers between devices with their start and end apart: 2 -> 2, of which waited for: 2 -> 2; matrix products, arithmetic and copies ran while one was open for 2% -> 1% of each run, Pallas kernels for 6% -> 7%
where the time goes in v3:
time: 156 us; the launch traced here: 155 us
  blocking collectives  59.7 us (38%)
  Pallas kernels  38.8 us (25%)
  waiting for transfers between devices  37.8 us (24%)
  starting transfers between devices  13.1 us (8%)
  local copies, waits for them, and re-layouts  5.79 us (4%)
    all_to_all x1, blocking collectives, body(): lax.all_to_all(moved, 'wide', split_axis=0, concat_axis=0, tiled=True)  45.3 us
    all_to_all x1, waiting for transfers between devices, body(): lax.all_to_all(moved, 'wide', split_axis=0, concat_axis=0, tiled=True)  29.3 us
    all_to_all x1, blocking collectives, body(): lax.all_to_all(moved, 'narrow', split_axis=0, concat_axis=0, tiled=True)  14.4 us
    pallas_call x1, Pallas kernels, cells_forward(): pl.pallas_call(forward_cells, in_specs=[pl.BlockSpec(memory_space=pl.ANY)...  10.5 us
    pallas_call x1, Pallas kernels, cells_backward(): pl.pallas_call(backward_cells, in_specs=[hbm, hbm, vmem, vmem, vmem, vmem...  10.1 us
    pallas_call x1, Pallas kernels, linear_part(): pl.pallas_call(linear_cells, in_specs=[pl.BlockSpec(memory_space=pl.ANY),...  9.61 us
    all_to_all x1, waiting for transfers between devices, body(): lax.all_to_all(moved, 'narrow', split_axis=0, concat_axis=0, tiled=True)  8.47 us
    all_to_all x1, starting transfers between devices, body(): lax.all_to_all(moved, 'wide', split_axis=0, concat_axis=0, tiled=True)  7.37 us
  transfers between devices with their start and end apart: 2, of which 2 were waited for; matrix products, arithmetic and copies ran while one was open for 1% of the time, Pallas kernels for 7%

profile of v3, /device:TPU:17, one launch (start us, length us, event | category | flops | bytes accessed | tf_op | source)
XLA Modules:
  0.0 155.4 jit_solution(3412309615794656696)
XLA Ops:
  0.0 10.5 %forward_cells.1 = f32[16,96,512]{2,1,0:T(8,128)} custom-call(f32[20,16,32,256]{3,2,1,0:T(8,128)} %x_ref.3, bf16[128,256]{1,0:T(8,128)(2,1)} %constant.20.clone.e_ref, bf16[352,256]{1,0:T(8,128)(2,1)} %constant.21.clone.zh_ref, bf16[352,256]{1,0:T(8,128)(2,1)} %constant.22.clone.zl_ref, f32[8,2,128]{2,1,0:T(2,128)} %constant.23.clone.phase_ref), custom_call_target="tpu_custom_call" | custom-call | tf_op jit(solution)/shard_map/forward_cells/pallas_call | solution.py:399
  10.5 0.0 copy-start.2
  10.5 0.0 copy-start.3
  10.5 45.3 %all_to_all.20.in_ref = f32[16,96,512]{2,1,0:T(8,128)S(1)} all-to-all(f32[16,96,512]{2,1,0:T(8,128)} %forward_cells.1), channel_id=1, replica_groups=mesh['wide'=16,'narrow'=8] {'wide'}, dimensions={0} | all-to-all | bytes 6291456 | tf_op jit(solution)/shard_map/all_to_all | solution.py:524
  55.8 0.0 copy-done.2
  55.8 0.0 copy-done.3
  55.8 2.6 %forward_rows.1 = f32[8,40,512]{2,1,0:T(8,128)} custom-call(bf16[320,1536]{1,0:T(8,128)(2,1)S(1)} %copy-done.3, bf16[320,1536]{1,0:T(8,128)(2,1)S(1)} %copy-done.2, f32[16,96,512]{2,1,0:T(8,128)S(1)} %all_to_all.20.in_ref), custom_call_target="tpu_custom_call" | custom-call | tf_op jit(solution)/shard_map/forward_rows/pallas_call | solution.py:424
  58.4 5.8 %all-to-all-start.1 = ((f32[8,40,512]{2,1,0:T(8,128)}), f32[8,40,512]{2,1,0:T(8,128)}, u32[]{:S(2)}, u32[]{:S(2)}) async-start(f32[8,40,512]{2,1,0:T(8,128)} %forward_rows.1), calls=%async_computation.1 | async-start | bytes 1310720 | tf_op jit(solution)/shard_map/all_to_all | solution.py:526
  64.1 0.0 copy-done.9
  64.1 0.9 copy.20
  65.0 1.0 arrange.1.w_ref
  66.0 8.5 %all-to-all-done.1.in_ref = f32[8,40,512]{2,1,0:T(8,128)} async-done(((f32[8,40,512]{2,1,0:T(8,128)}), f32[8,40,512]{2,1,0:T(8,128)}, u32[]{:S(2)}, u32[]{:S(2)}) %all-to-all-start.1) | async-done | bytes 655392 | tf_op jit(solution)/shard_map/all_to_all | solution.py:526
  74.5 2.0 %mix.1 = f32[8,40,512]{2,1,0:T(8,128)S(1)} custom-call(f32[8,40,512]{2,1,0:T(8,128)} %all-to-all-done.1.in_ref, f32[20,20,8,256]{3,2,1,0:T(8,128)S(1)} %arrange.1.w_ref), custom_call_target="tpu_custom_call" | custom-call | tf_op jit(solution)/shard_map/mix/pallas_call | solution.py:445
  76.4 14.4 %all_to_all.21.in_ref = f32[8,40,512]{2,1,0:T(8,128)S(1)} all-to-all(f32[8,40,512]{2,1,0:T(8,128)S(1)} %mix.1), channel_id=1, replica_groups=mesh['wide'=16,'narrow'=8] {'narrow'}, dimensions={0} | all-to-all | bytes 1310720 | tf_op jit(solution)/shard_map/all_to_all | solution.py:528
  90.9 0.0 copy-done.1
  90.9 3.1 %backward_rows.1 = f32[16,96,512]{2,1,0:T(8,128)} custom-call(bf16[1536,960]{1,0:T(8,128)(2,1)S(1)} %copy-done.1, f32[8,40,512]{2,1,0:T(8,128)S(1)} %all_to_all.21.in_ref), custom_call_target="tpu_custom_call" | custom-call | tf_op jit(solution)/shard_map/backward_rows/pallas_call | solution.py:455
  94.0 7.4 %all-to-all-start.3 = ((f32[16,96,512]{2,1,0:T(8,128)}), f32[16,96,512]{2,1,0:T(8,128)S(1)}, u32[]{:S(2)}, u32[]{:S(2)}) async-start(f32[16,96,512]{2,1,0:T(8,128)} %backward_rows.1), calls=%async_computation.3 | async-start | bytes 6291456 | tf_op jit(solution)/shard_map/all_to_all | solution.py:530
  101.4 0.0 copy-done.10
  101.4 0.0 copy-done.8
  101.4 0.0 copy-start.4
  101.4 0.0 copy-start.5
  101.4 0.0 copy-start.7
  101.4 9.6 %linear_cells.1.linear_ref = f32[20,16,32,256]{3,2,1,0:T(8,128)S(1)} custom-call(f32[20,16,32,256]{3,2,1,0:T(8,128)} %x_ref.3, f32[20,20]{1,0:T(8,128)S(1)} %bitcast.7, f32[1,20]{1,0:T(1,128)S(1)} %copy-done.8), custom_call_target="tpu_custom_call" | custom-call | flops 2516582400 | bytes 20971520 | tf_op jit(solution)/shard_map/linear_cells/pallas_call | solution.py:470
  111.1 0.0 copy-start
  111.1 4.0 %copy-done = f32[20,16,32,256]{3,2,1,0:T(8,128)} copy-done((f32[20,16,32,256]{3,2,1,0:T(8,128)}, f32[20,16,32,256]{3,2,1,0:T(8,128)S(1)}, u32[]{:S(2)}) %copy-start) | copy-done | bytes 10485784
  115.0 29.3 %all-to-all-done.3.in_ref = f32[16,96,512]{2,1,0:T(8,128)S(1)} async-done(((f32[16,96,512]{2,1,0:T(8,128)}), f32[16,96,512]{2,1,0:T(8,128)S(1)}, u32[]{:S(2)}, u32[]{:S(2)}) %all-to-all-start.3) | async-done | bytes 3145760 | tf_op jit(solution)/shard_map/all_to_all | solution.py:530
  144.4 0.0 copy-done.4
  144.4 0.0 copy-done.5
  144.4 0.0 copy-done.7
  144.4 0.0 copy-start.6
  144.4 0.9 copy-done.6
  145.3 10.1 %backward_cells.1 = f32[20,16,32,256]{3,2,1,0:T(8,128)} custom-call(f32[20,16,32,256]{3,2,1,0:T(8,128)} %copy-done, f32[16,96,512]{2,1,0:T(8,128)S(1)} %all-to-all-done.3.in_ref, bf16[256,256]{1,0:T(8,128)(2,1)S(1)} %copy-done.6, bf16[352,256]{1,0:T(8,128)(2,1)S(1)} %copy-done.5, bf16[352,256]{1,0:T(8,128)(2,1)S(1)} %copy-done.4, f32[8,2,128]{2,1,0:T(2,128)S(1)} %copy-done.7), custom_call_target="tpu_custom_call" | custom-call | tf_op jit(solution)/shard_map/backward_cells/pallas_call | solution.py:503
  (5 shorter events, 0.0 us)
Async XLA Ops:
  10.5 45.3 %copy-start.2 = (bf16[320,1536]{1,0:T(8,128)(2,1)S(1)}, bf16[320,1536]{1,0:T(8,128)(2,1)}, u32[]{:S(2)}) copy-start(bf16[320,1536]{1,0:T(8,128)(2,1)} %constant.25.clone.low_ref) | copy-start | bytes 2949124
  10.5 45.3 %copy-start.3 = (bf16[320,1536]{1,0:T(8,128)(2,1)S(1)}, bf16[320,1536]{1,0:T(8,128)(2,1)}, u32[]{:S(2)}) copy-start(bf16[320,1536]{1,0:T(8,128)(2,1)} %constant.24.clone.high_ref) | copy-start | bytes 2949124
  55.8 8.3 %copy-start.9 = (f32[1,2,20,20,3,144]{5,1,4,3,2,0:T(2,128)S(1)}, f32[1,2,20,20,3,144]{5,1,4,3,2,0:T(2,128)}, u32[]{:S(2)}) copy-start(f32[1,2,20,20,3,144]{5,1,4,3,2,0:T(2,128)} %param.16) | copy-start | bytes 4147204
  58.4 16.1 %all-to-all-start.1 = ((f32[8,40,512]{2,1,0:T(8,128)}), f32[8,40,512]{2,1,0:T(8,128)}, u32[]{:S(2)}, u32[]{:S(2)}) async-start(f32[8,40,512]{2,1,0:T(8,128)} %forward_rows.1), calls=%async_computation.1 | async-start | bytes 1310720 | tf_op jit(solution)/shard_map/all_to_all | solution.py:526
  74.5 16.4 %copy-start.1 = (bf16[1536,960]{1,0:T(8,128)(2,1)S(1)}, bf16[1536,960]{1,0:T(8,128)(2,1)}, u32[]{:S(2)}) copy-start(bf16[1536,960]{1,0:T(8,128)(2,1)} %constant.26.clone.table_ref) | copy-start | bytes 8847364
  94.0 7.4 %copy-start.10 = (f32[1,20,20]{2,0,1:T(1,128)S(1)}, f32[1,20,20]{2,0,1:T(1,128)}, u32[]{:S(2)}) copy-start(f32[1,20,20]{2,0,1:T(1,128)} %param.17) | copy-start | bytes 4804
  94.0 7.4 %copy-start.8 = (f32[1,20]{1,0:T(1,128)S(1)}, f32[1,20]{1,0:T(1,128)}, u32[]{:S(2)}) copy-start(f32[1,20]{1,0:T(1,128)} %bias_ref.1) | copy-start | bytes 244
  94.0 50.4 %all-to-all-start.3 = ((f32[16,96,512]{2,1,0:T(8,128)}), f32[16,96,512]{2,1,0:T(8,128)S(1)}, u32[]{:S(2)}, u32[]{:S(2)}) async-start(f32[16,96,512]{2,1,0:T(8,128)} %backward_rows.1), calls=%async_computation.3 | async-start | bytes 6291456 | tf_op jit(solution)/shard_map/all_to_all | solution.py:530
  101.4 43.0 %copy-start.4 = (bf16[352,256]{1,0:T(8,128)(2,1)S(1)}, bf16[352,256]{1,0:T(8,128)(2,1)}, u32[]{:S(2)}) copy-start(bf16[352,256]{1,0:T(8,128)(2,1)} %constant.29.clone.zl_ref) | copy-start | bytes 540676
  101.4 43.0 %copy-start.5 = (bf16[352,256]{1,0:T(8,128)(2,1)S(1)}, bf16[352,256]{1,0:T(8,128)(2,1)}, u32[]{:S(2)}) copy-start(bf16[352,256]{1,0:T(8,128)(2,1)} %constant.28.clone.zh_ref) | copy-start | bytes 540676
  101.4 43.0 %copy-start.7 = (f32[8,2,128]{2,1,0:T(2,128)S(1)}, f32[8,2,128]{2,1,0:T(2,128)}, u32[]{:S(2)}) copy-start(f32[8,2,128]{2,1,0:T(2,128)} %constant.23.clone.phase_ref) | copy-start | bytes 24580
  111.1 4.0 %copy-start = (f32[20,16,32,256]{3,2,1,0:T(8,128)}, f32[20,16,32,256]{3,2,1,0:T(8,128)S(1)}, u32[]{:S(2)}) copy-start(f32[20,16,32,256]{3,2,1,0:T(8,128)S(1)} %linear_cells.1.linear_ref) | copy-start | bytes 31457284
  144.4 0.9 copy-start.6

commit v4 on v3

--- a/solution.py
+++ b/solution.py
@@ -57,8 +57,8 @@
     return table
 
 
-def window_of(ref, group):
-    return ref[96 - 32 * group : 352 - 32 * group]
+def window_of(ref, group, base=0):
+    return ref[base + 96 - 32 * group : base + 352 - 32 * group]
 
 
 def phase_table():
@@ -289,7 +289,7 @@
 
 
 def backward_cells(
-    linear_ref, in_ref, e_ref, zh_ref, zl_ref, phase_ref, out_ref,
+    linear_ref, in_ref, table_ref, phase_ref, out_ref,
     x_buf, in_buf, out_buf, cell_ref, x_sem, in_sem, out_sem,
 ):
     def modes_in(half):
@@ -349,7 +349,7 @@
             u, v = turn_c * u - turn_s * v, turn_s * u + turn_c * v
             cells = dot3(
                 split(jnp.concatenate([u, v], axis=1)),
-                (window_of(zh_ref, group), window_of(zl_ref, group)),
+                (window_of(table_ref, group), window_of(table_ref, group, 352)),
                 ((1,), (1,)),
             )
             left, right = cells[:, :128], cells[:, 128:]
@@ -363,7 +363,7 @@
                 [cell_ref[tile, pl.ds(row, 64, stride=8), :] for tile in range(5)], axis=1
             )
             pair = jnp.transpose(jnp.concatenate(split(seqs), axis=0))
-            spatial = dot(jnp.concatenate([pair, pair], axis=1), e_ref[...])
+            spatial = dot(jnp.concatenate([pair, pair], axis=1), table_ref[704:960])
             fetch(y).wait()
 
             @pl.when(y + AHEAD < 16)
@@ -502,7 +502,7 @@
     hbm = pl.BlockSpec(memory_space=pl.ANY)
     return pl.pallas_call(
         backward_cells,
-        in_specs=[hbm, hbm, vmem, vmem, vmem, vmem],
+        in_specs=[hbm, hbm, vmem, vmem],
         out_specs=hbm,
         out_shape=jax.ShapeDtypeStruct(linear.shape, f32),
         scratch_shapes=[
@@ -516,7 +516,7 @@
         ],
         compiler_params=pltpu.CompilerParams(vmem_limit_bytes=46 * 1024 * 1024),
         name="backward_cells",
-    )(linear, moved, np.concatenate([eh, eh, el, np.zeros_like(el)]), zh, zl, phase_table())
+    )(linear, moved, np.concatenate([zh, zl, eh, eh, el, np.zeros_like(el)]), phase_table())
 
 
 def body(field, spec_weight, lin_weight, bias):

time: 156 us -> 156 us (level)
    unnamed x24 -> x20, local copies, waits for them, and re-layouts: 5.79 us -> 5.89 us
where the time goes in v4:
time: 156 us; the launch traced here: 155 us
  blocking collectives  59.7 us (38%)
  Pallas kernels  38.8 us (25%)
  waiting for transfers between devices  37.8 us (24%)
  starting transfers between devices  13.1 us (8%)
  local copies, waits for them, and re-layouts  5.89 us (4%)
    all_to_all x1, blocking collectives, body(): lax.all_to_all(moved, 'wide', split_axis=0, concat_axis=0, tiled=True)  45.3 us
    all_to_all x1, waiting for transfers between devices, body(): lax.all_to_all(moved, 'wide', split_axis=0, concat_axis=0, tiled=True)  29.4 us
    all_to_all x1, blocking collectives, body(): lax.all_to_all(moved, 'narrow', split_axis=0, concat_axis=0, tiled=True)  14.4 us
    pallas_call x1, Pallas kernels, cells_forward(): pl.pallas_call(forward_cells, in_specs=[pl.BlockSpec(memory_space=pl.ANY)...  10.5 us
    pallas_call x1, Pallas kernels, cells_backward(): pl.pallas_call(backward_cells, in_specs=[hbm, hbm, vmem, vmem], out_specs...  10.1 us
    pallas_call x1, Pallas kernels, linear_part(): pl.pallas_call(linear_cells, in_specs=[pl.BlockSpec(memory_space=pl.ANY),...  9.61 us
    all_to_all x1, waiting for transfers between devices, body(): lax.all_to_all(moved, 'narrow', split_axis=0, concat_axis=0, tiled=True)  8.47 us
    all_to_all x1, starting transfers between devices, body(): lax.all_to_all(moved, 'wide', split_axis=0, concat_axis=0, tiled=True)  7.37 us
  transfers between devices with their start and end apart: 2, of which 2 were waited for; matrix products, arithmetic and copies ran while one was open for 1% of the time, Pallas kernels for 7%

profile of v4, /device:TPU:17, one launch (start us, length us, event | category | flops | bytes accessed | tf_op | source)
XLA Modules:
  0.0 155.5 jit_solution(8808217361083530921)
XLA Ops:
  0.0 10.5 %forward_cells.1 = f32[16,96,512]{2,1,0:T(8,128)} custom-call(f32[20,16,32,256]{3,2,1,0:T(8,128)} %x_ref.3, bf16[128,256]{1,0:T(8,128)(2,1)} %constant.16.clone.e_ref, bf16[352,256]{1,0:T(8,128)(2,1)} %constant.17.clone.zh_ref, bf16[352,256]{1,0:T(8,128)(2,1)} %constant.18.clone.zl_ref, f32[8,2,128]{2,1,0:T(2,128)} %constant.19.clone.phase_ref), custom_call_target="tpu_custom_call" | custom-call | tf_op jit(solution)/shard_map/forward_cells/pallas_call | solution.py:399
  10.5 0.0 copy-start.2
  10.5 0.0 copy-start.3
  10.5 45.3 %all_to_all.20.in_ref = f32[16,96,512]{2,1,0:T(8,128)S(1)} all-to-all(f32[16,96,512]{2,1,0:T(8,128)} %forward_cells.1), channel_id=1, replica_groups=mesh['wide'=16,'narrow'=8] {'wide'}, dimensions={0} | all-to-all | bytes 6291456 | tf_op jit(solution)/shard_map/all_to_all | solution.py:524
  55.8 0.0 copy-done.2
  55.8 0.0 copy-done.3
  55.8 0.0 copy-start.7
  55.8 2.6 %forward_rows.1 = f32[8,40,512]{2,1,0:T(8,128)} custom-call(bf16[320,1536]{1,0:T(8,128)(2,1)S(1)} %copy-done.3, bf16[320,1536]{1,0:T(8,128)(2,1)S(1)} %copy-done.2, f32[16,96,512]{2,1,0:T(8,128)S(1)} %all_to_all.20.in_ref), custom_call_target="tpu_custom_call" | custom-call | tf_op jit(solution)/shard_map/forward_rows/pallas_call | solution.py:424
  58.4 5.8 %all-to-all-start.1 = ((f32[8,40,512]{2,1,0:T(8,128)}), f32[8,40,512]{2,1,0:T(8,128)}, u32[]{:S(2)}, u32[]{:S(2)}) async-start(f32[8,40,512]{2,1,0:T(8,128)} %forward_rows.1), calls=%async_computation.1 | async-start | bytes 1310720 | tf_op jit(solution)/shard_map/all_to_all | solution.py:526
  64.1 0.0 copy-done.7
  64.1 0.9 copy.18
  65.0 1.0 arrange.1.w_ref
  66.0 8.5 %all-to-all-done.1.in_ref = f32[8,40,512]{2,1,0:T(8,128)} async-done(((f32[8,40,512]{2,1,0:T(8,128)}), f32[8,40,512]{2,1,0:T(8,128)}, u32[]{:S(2)}, u32[]{:S(2)}) %all-to-all-start.1) | async-done | bytes 655392 | tf_op jit(solution)/shard_map/all_to_all | solution.py:526
  74.5 0.0 copy-start.1
  74.5 2.0 %mix.1 = f32[8,40,512]{2,1,0:T(8,128)S(1)} custom-call(f32[8,40,512]{2,1,0:T(8,128)} %all-to-all-done.1.in_ref, f32[20,20,8,256]{3,2,1,0:T(8,128)S(1)} %arrange.1.w_ref), custom_call_target="tpu_custom_call" | custom-call | tf_op jit(solution)/shard_map/mix/pallas_call | solution.py:445
  76.4 14.4 %all_to_all.21.in_ref = f32[8,40,512]{2,1,0:T(8,128)S(1)} all-to-all(f32[8,40,512]{2,1,0:T(8,128)S(1)} %mix.1), channel_id=1, replica_groups=mesh['wide'=16,'narrow'=8] {'narrow'}, dimensions={0} | all-to-all | bytes 1310720 | tf_op jit(solution)/shard_map/all_to_all | solution.py:528
  90.9 0.0 copy-done.1
  90.9 3.1 %backward_rows.1 = f32[16,96,512]{2,1,0:T(8,128)} custom-call(bf16[1536,960]{1,0:T(8,128)(2,1)S(1)} %copy-done.1, f32[8,40,512]{2,1,0:T(8,128)S(1)} %all_to_all.21.in_ref), custom_call_target="tpu_custom_call" | custom-call | tf_op jit(solution)/shard_map/backward_rows/pallas_call | solution.py:455
  94.0 0.0 copy-start.8
  94.0 0.0 copy-start.6
  94.0 7.4 %all-to-all-start.3 = ((f32[16,96,512]{2,1,0:T(8,128)}), f32[16,96,512]{2,1,0:T(8,128)S(1)}, u32[]{:S(2)}, u32[]{:S(2)}) async-start(f32[16,96,512]{2,1,0:T(8,128)} %backward_rows.1), calls=%async_computation.3 | async-start | bytes 6291456 | tf_op jit(solution)/shard_map/all_to_all | solution.py:530
  101.4 0.0 copy-done.8
  101.4 0.0 copy-done.6
  101.4 0.0 copy-start.5
  101.4 9.6 %linear_cells.1.linear_ref = f32[20,16,32,256]{3,2,1,0:T(8,128)S(1)} custom-call(f32[20,16,32,256]{3,2,1,0:T(8,128)} %x_ref.3, f32[20,20]{1,0:T(8,128)S(1)} %bitcast.7, f32[1,20]{1,0:T(1,128)S(1)} %copy-done.6), custom_call_target="tpu_custom_call" | custom-call | flops 2516582400 | bytes 20971520 | tf_op jit(solution)/shard_map/linear_cells/pallas_call | solution.py:470
  111.0 0.0 copy-start
  111.0 4.0 %copy-done = f32[20,16,32,256]{3,2,1,0:T(8,128)} copy-done((f32[20,16,32,256]{3,2,1,0:T(8,128)}, f32[20,16,32,256]{3,2,1,0:T(8,128)S(1)}, u32[]{:S(2)}) %copy-start) | copy-done | bytes 10485784
  115.0 29.4 %all-to-all-done.3.in_ref = f32[16,96,512]{2,1,0:T(8,128)S(1)} async-done(((f32[16,96,512]{2,1,0:T(8,128)}), f32[16,96,512]{2,1,0:T(8,128)S(1)}, u32[]{:S(2)}, u32[]{:S(2)}) %all-to-all-start.3) | async-done | bytes 3145760 | tf_op jit(solution)/shard_map/all_to_all | solution.py:530
  144.4 0.0 copy-done.5
  144.4 0.0 copy-start.4
  144.4 1.0 copy-done.4
  145.4 10.1 %backward_cells.1 = f32[20,16,32,256]{3,2,1,0:T(8,128)} custom-call(f32[20,16,32,256]{3,2,1,0:T(8,128)} %copy-done, f32[16,96,512]{2,1,0:T(8,128)S(1)} %all-to-all-done.3.in_ref, bf16[960,256]{1,0:T(8,128)(2,1)S(1)} %copy-done.4, f32[8,2,128]{2,1,0:T(2,128)S(1)} %copy-done.5), custom_call_target="tpu_custom_call" | custom-call | tf_op jit(solution)/shard_map/backward_cells/pallas_call | solution.py:503
  (1 shorter events, 0.0 us)
Async XLA Ops:
  10.5 45.3 %copy-start.2 = (bf16[320,1536]{1,0:T(8,128)(2,1)S(1)}, bf16[320,1536]{1,0:T(8,128)(2,1)}, u32[]{:S(2)}) copy-start(bf16[320,1536]{1,0:T(8,128)(2,1)} %constant.21.clone.low_ref) | copy-start | bytes 2949124
  10.5 45.3 %copy-start.3 = (bf16[320,1536]{1,0:T(8,128)(2,1)S(1)}, bf16[320,1536]{1,0:T(8,128)(2,1)}, u32[]{:S(2)}) copy-start(bf16[320,1536]{1,0:T(8,128)(2,1)} %constant.20.clone.high_ref) | copy-start | bytes 2949124
  55.8 8.3 %copy-start.7 = (f32[1,2,20,20,3,144]{5,1,4,3,2,0:T(2,128)S(1)}, f32[1,2,20,20,3,144]{5,1,4,3,2,0:T(2,128)}, u32[]{:S(2)}) copy-start(f32[1,2,20,20,3,144]{5,1,4,3,2,0:T(2,128)} %param.14) | copy-start | bytes 4147204
  58.4 16.1 %all-to-all-start.1 = ((f32[8,40,512]{2,1,0:T(8,128)}), f32[8,40,512]{2,1,0:T(8,128)}, u32[]{:S(2)}, u32[]{:S(2)}) async-start(f32[8,40,512]{2,1,0:T(8,128)} %forward_rows.1), calls=%async_computation.1 | async-start | bytes 1310720 | tf_op jit(solution)/shard_map/all_to_all | solution.py:526
  74.5 16.4 %copy-start.1 = (bf16[1536,960]{1,0:T(8,128)(2,1)S(1)}, bf16[1536,960]{1,0:T(8,128)(2,1)}, u32[]{:S(2)}) copy-start(bf16[1536,960]{1,0:T(8,128)(2,1)} %constant.22.clone.table_ref) | copy-start | bytes 8847364
  94.0 7.4 %copy-start.8 = (f32[1,20,20]{2,0,1:T(1,128)S(1)}, f32[1,20,20]{2,0,1:T(1,128)}, u32[]{:S(2)}) copy-start(f32[1,20,20]{2,0,1:T(1,128)} %param.15) | copy-start | bytes 4804
  94.0 7.4 %copy-start.6 = (f32[1,20]{1,0:T(1,128)S(1)}, f32[1,20]{1,0:T(1,128)}, u32[]{:S(2)}) copy-start(f32[1,20]{1,0:T(1,128)} %bias_ref.1) | copy-start | bytes 244
  94.0 50.4 %all-to-all-start.3 = ((f32[16,96,512]{2,1,0:T(8,128)}), f32[16,96,512]{2,1,0:T(8,128)S(1)}, u32[]{:S(2)}, u32[]{:S(2)}) async-start(f32[16,96,512]{2,1,0:T(8,128)} %backward_rows.1), calls=%async_computation.3 | async-start | bytes 6291456 | tf_op jit(solution)/shard_map/all_to_all | solution.py:530
  101.4 43.0 %copy-start.5 = (f32[8,2,128]{2,1,0:T(2,128)S(1)}, f32[8,2,128]{2,1,0:T(2,128)}, u32[]{:S(2)}) copy-start(f32[8,2,128]{2,1,0:T(2,128)} %constant.19.clone.phase_ref) | copy-start | bytes 24580
  111.0 4.0 %copy-start = (f32[20,16,32,256]{3,2,1,0:T(8,128)}, f32[20,16,32,256]{3,2,1,0:T(8,128)S(1)}, u32[]{:S(2)}) copy-start(f32[20,16,32,256]{3,2,1,0:T(8,128)S(1)} %linear_cells.1.linear_ref) | copy-start | bytes 31457284
  144.4 1.0 copy-start.4
